TPU v7x, 128 devices: a whole 4x4x4 slice. The times are simulated.
128 devices in a mesh: pipe: 4 (over z), ed: 32 (over y, x, core).
Axes of the slice: x: 4, y: 4, z: 4, core: 2. Of those that a mesh axis runs over, the one named last changes fastest.
Arguments:
- inputs: bfloat16 [8, 512, 6144], P(None, 'ed', 'pipe'), may hold values from -6 to 6
- gain: bfloat16 [4, 6144], P('pipe'), may hold values from 0.5 to 1.5
- w_up: bfloat16 [4, 6144, 32768], P('pipe', None, 'ed'), may hold values from -0.078125 to 0.078125
- w_down: bfloat16 [4, 32768, 6144], P('pipe', 'ed'), may hold values from -0.0625 to 0.0625
- routes: int32 [4, 8, 512, 2], P('pipe', None, 'ed'), may hold values from 0 to 7, all different within a row; in each aligned block of 16 rows (0 to 15, 16 to 31, ..., all dimensions but the last counted through in order) at most 6 rows name the same one
- route_weight: float32 [4, 8, 512, 2], P('pipe', None, 'ed'), may hold values from 0.1 to 0.9
Outputs:
- hidden_states: bfloat16 [4, 8, 512, 6144], P('pipe', None, 'ed')
Inputs may be any that keep to these rules, and one draw needn't show every extreme that they name: `routes`: the two experts of a token differ. In each micro-batch of each section, the 16 tokens of one device name no expert more than 6 times; in some micro-batches an expert is named exactly 6 times there.
All inputs are finite; a program needn't handle non-finite values.
Results may differ from a plain program's by a relative error of at most 0.0095.
Values may be sent and summed in bfloat16 or wider, within the bound.
No kernel may reach another device: no remote copies, remote signals or barrier semaphores. Data moves between devices by JAX's collectives and lax.ppermute only.
A program may use at most 128 MiB of HBM per device.

v0:
```python
import jax
import jax.numpy as jnp
from jax import lax
from jax.sharding import PartitionSpec as P

EXPERTS = 4
MOST = 6


def passed_along(value, axis, by):
    devices = lax.axis_size(axis)
    pairs = [(i, i + by) for i in range(devices) if 0 <= i + by < devices]
    return lax.ppermute(value, axis, pairs)


def rank_within(chosen, experts):
    flat = chosen.reshape(-1)
    onehot = (flat[:, None] == jnp.arange(experts, dtype=jnp.int32)[None, :]).astype(jnp.int32)
    before = jnp.cumsum(onehot, axis=0) - onehot
    return jnp.sum(before * onehot, axis=1).reshape(chosen.shape)


def expert_rows(rows, up_local, down_local):
    hidden = jax.nn.silu(jnp.dot(rows, up_local, preferred_element_type=jnp.float32)).astype(
        jnp.bfloat16
    )
    return jnp.dot(hidden, down_local, preferred_element_type=jnp.float32).astype(jnp.bfloat16)


def on_device(inputs, gain, w_up, w_down, routes, route_weight):
    whole_inputs = lax.all_gather(inputs, "pipe", axis=2, tiled=True)
    micro, tok, width = whole_inputs.shape
    n_ed = lax.axis_size("ed")
    n_pipe = lax.axis_size("pipe")
    experts = EXPERTS
    group = n_ed // experts
    most = MOST
    slots = n_ed * most
    padded_rows = (slots + 127) // 128 * 128
    segment = lax.axis_index("pipe")
    up_local = w_up[0]
    down_local = w_down[0]
    gain_local = gain[0].astype(jnp.float32)

    def section(panel, step_micro):
        values = panel.astype(jnp.float32)
        scale = lax.rsqrt(jnp.mean(values * values, axis=-1, keepdims=True) + 1e-05)
        normed = (values * scale * gain_local).astype(jnp.bfloat16)
        chosen = lax.dynamic_index_in_dim(routes[0], step_micro, 0, keepdims=False)
        weights = lax.dynamic_index_in_dim(route_weight[0], step_micro, 0, keepdims=False)
        inside = chosen < experts
        my_slot = jnp.where(inside, chosen * most + rank_within(chosen, experts), experts * most)
        slot_ids = jnp.arange(experts * most, dtype=jnp.int32)[:, None]
        table = ((slot_ids == my_slot[None, :, 0]) | (slot_ids == my_slot[None, :, 1])).astype(
            jnp.bfloat16
        )
        packed = jnp.dot(table, normed, preferred_element_type=jnp.float32).astype(jnp.bfloat16)
        outgoing = jnp.broadcast_to(
            packed.reshape(experts, 1, most, width), (experts, group, most, width)
        )
        expert_ids = jnp.arange(experts, dtype=jnp.int32)[:, None, None]
        named_count = jnp.sum((chosen[None, :, :] == expert_ids).astype(jnp.float32), axis=(1, 2))
        count_out = (
            jnp.broadcast_to(named_count[:, None], (experts, group))
            .reshape(n_ed, 1)
            .astype(jnp.bfloat16)
        )
        received, count_in = (
            lax.all_to_all(
                outgoing.reshape(n_ed, most, width), "ed", split_axis=0, concat_axis=0, tiled=True
            ),
            lax.all_to_all(count_out, "ed", split_axis=0, concat_axis=0, tiled=True),
        )
        received = received.reshape(slots, width)
        counts = count_in[:, 0].astype(jnp.int32)
        inclusive = jnp.cumsum(counts)
        exclusive = inclusive - counts
        live = inclusive[-1]
        row_ids = jnp.arange(padded_rows, dtype=jnp.int32)
        source_of = jnp.minimum(
            jnp.sum((inclusive[None, :] <= row_ids[:, None]).astype(jnp.int32), axis=1), n_ed - 1
        )
        within = jnp.clip(row_ids - exclusive[source_of], 0, most - 1)
        compact = jnp.take(received, source_of * most + within, axis=0)

        def one_block(block, done):
            rows = lax.dynamic_slice_in_dim(compact, block * 128, 128, 0)
            return lax.dynamic_update_slice_in_dim(
                done, expert_rows(rows, up_local, down_local), block * 128, 0
            )

        done = lax.fori_loop(
            0, (live + 127) // 128, one_block, jnp.zeros((padded_rows, width), jnp.bfloat16)
        )
        position = jnp.arange(most, dtype=jnp.int32)[None, :]
        back_index = jnp.minimum(exclusive[:, None] + position, padded_rows - 1)
        live_mask = position < counts[:, None]
        returned = jnp.take(done, back_index.reshape(-1), axis=0).reshape(n_ed, most, width)
        returned = jnp.where(live_mask[:, :, None], returned, jnp.zeros_like(returned))
        partials = lax.all_to_all(returned, "ed", split_axis=0, concat_axis=0, tiled=True)
        summed = jnp.sum(partials.reshape(experts, group, most, width), axis=1, dtype=jnp.float32)
        summed = summed.reshape(experts * most, width)
        safe_slot = jnp.minimum(my_slot, experts * most - 1)
        weight_used = jnp.where(inside, weights, jnp.zeros_like(weights))
        mixed = weight_used[:, 0:1] * jnp.take(summed, safe_slot[:, 0], axis=0)
        mixed = mixed + weight_used[:, 1:2] * jnp.take(summed, safe_slot[:, 1], axis=0)
        return (values + mixed).astype(jnp.bfloat16)

    def one_step(step, state):
        carried, result = state
        offset = step - segment
        active = (offset >= 0) & (offset < micro)
        step_micro = jnp.clip(offset, 0, micro - 1)
        first = lax.dynamic_index_in_dim(whole_inputs, step_micro, 0, keepdims=False)
        panel = jnp.where(segment == 0, first, carried)
        produced = section(panel, step_micro)
        produced = jnp.where(active, produced, jnp.zeros_like(produced))
        result = jnp.where(
            active, lax.dynamic_update_index_in_dim(result, produced, step_micro, 0), result
        )
        carried = passed_along(produced, "pipe", 1)
        return (carried, result)

    start_state = (
        jnp.zeros((tok, width), jnp.bfloat16),
        jnp.zeros((micro, tok, width), jnp.bfloat16),
    )
    final_state = lax.fori_loop(0, micro + n_pipe - 1, one_step, start_state)
    return final_state[1][None]


def solution(mesh):
    in_specs = (
        P(None, "ed", "pipe"),
        P("pipe", None),
        P("pipe", None, "ed"),
        P("pipe", "ed", None),
        P("pipe", None, "ed", None),
        P("pipe", None, "ed", None),
    )
    out_specs = P("pipe", None, "ed", None)
    return jax.shard_map(
        on_device, mesh=mesh, in_specs=in_specs, out_specs=out_specs, check_vma=False
    )
```

profile of v0, /device:TPU:1, one launch (start us, length us, event | category | flops | bytes accessed | tf_op | source)
XLA Modules:
  0.0 1823.8 jit_solution(10903924219914020317)
XLA Ops:
  8.6 30.4 %all-gather.2.cloned.1.call-done = bf16[8,16,6144]{2,1,0:T(8,128)(2,1)} async-done(((bf16[8,16,1536]{2,1,0:T(8,128)(2,1)}), bf16[8,16,6144]{2,1,0:T(8,128)(2,1)}) %all-gather.2.cloned.1.call-update) | async-done | bytes 1572880 | tf_op jit(solution)/shard_map/all_gather | solution.py:31
  40.3 1776.7 %while.49 = (s32[]{:T(128)}, bf16[16,6144]{1,0:T(8,128)(2,1)S(1)}, bf16[8,16,6144]{2,1,0:T(8,128)(2,1)}, s32[]{:T(128)}, pred[]{:T(512)}, /*index=5*/bf16[8,16,6...) while((s32[]{:T(128)}, bf16[16,6144]{1,0:T(8,128)(2,1)S(1)}, ...), condition=%wide.region_10.12_spmd, body=%wide.region_0.11_spmd.sunk | while | flops 3235507200 | bytes 143577904 | solution.py:128
  87.3 15.5 all-to-all-done.1
  114.2 21.0 %while.50 = (s32[]{:T(128)}, bf16[256,6144]{1,0:T(8,128)(2,1)S(1)}, s32[]{:T(128)}, bf16[256,6144]{1,0:T(8,128)(2,1)}, bf16[6144,1024]{1,0:T(8,128)(2,1)}, /*ind...) while((s32[]{:T(128)}, bf16[256,6144]{1,0:T(8,128)(2,1)S(1)}, s32[]{:T(128)}, ...), condition=%wide.region_8.8_spmd, body=%wide.region_7.7_spmd.sunk | while | flops 3222667264 | bytes 79167672 | solution.py:92
  150.3 39.2 %all-to-all-done.2 = bf16[32,6,6144]{2,1,0:T(8,128)(2,1)S(1)} async-done(((bf16[32,6,6144]{2,1,0:T(8,128)(2,1)}), bf16[32,6,6144]{2,1,0:T(8,128)(2,1)S(1)}, u32[]{:S(2)}, u32[]{:S(2)}) %all-to-all-start.2) | async-done | bytes 2359328 | tf_op jit(solution)/shard_map/while/body/eval_jaxpr/all_to_all | solution.py:100
  247.0 15.5 all-to-all-done.1
  273.8 21.0 %while.50 = (s32[]{:T(128)}, bf16[256,6144]{1,0:T(8,128)(2,1)S(1)}, s32[]{:T(128)}, bf16[256,6144]{1,0:T(8,128)(2,1)}, bf16[6144,1024]{1,0:T(8,128)(2,1)}, /*ind...) while((s32[]{:T(128)}, bf16[256,6144]{1,0:T(8,128)(2,1)S(1)}, s32[]{:T(128)}, ...), condition=%wide.region_8.8_spmd, body=%wide.region_7.7_spmd.sunk | while | flops 3222667264 | bytes 79167672 | solution.py:92
  309.9 39.2 %all-to-all-done.2 = bf16[32,6,6144]{2,1,0:T(8,128)(2,1)S(1)} async-done(((bf16[32,6,6144]{2,1,0:T(8,128)(2,1)}), bf16[32,6,6144]{2,1,0:T(8,128)(2,1)S(1)}, u32[]{:S(2)}, u32[]{:S(2)}) %all-to-all-start.2) | async-done | bytes 2359328 | tf_op jit(solution)/shard_map/while/body/eval_jaxpr/all_to_all | solution.py:100
  435.5 21.0 %while.50 = (s32[]{:T(128)}, bf16[256,6144]{1,0:T(8,128)(2,1)S(1)}, s32[]{:T(128)}, bf16[256,6144]{1,0:T(8,128)(2,1)}, bf16[6144,1024]{1,0:T(8,128)(2,1)}, /*ind...) while((s32[]{:T(128)}, bf16[256,6144]{1,0:T(8,128)(2,1)S(1)}, s32[]{:T(128)}, ...), condition=%wide.region_8.8_spmd, body=%wide.region_7.7_spmd.sunk | while | flops 3222667264 | bytes 79167672 | solution.py:92
  471.6 39.2 %all-to-all-done.2 = bf16[32,6,6144]{2,1,0:T(8,128)(2,1)S(1)} async-done(((bf16[32,6,6144]{2,1,0:T(8,128)(2,1)}), bf16[32,6,6144]{2,1,0:T(8,128)(2,1)S(1)}, u32[]{:S(2)}, u32[]{:S(2)}) %all-to-all-start.2) | async-done | bytes 2359328 | tf_op jit(solution)/shard_map/while/body/eval_jaxpr/all_to_all | solution.py:100
  570.3 15.5 all-to-all-done.1
  597.2 21.0 %while.50 = (s32[]{:T(128)}, bf16[256,6144]{1,0:T(8,128)(2,1)S(1)}, s32[]{:T(128)}, bf16[256,6144]{1,0:T(8,128)(2,1)}, bf16[6144,1024]{1,0:T(8,128)(2,1)}, /*ind...) while((s32[]{:T(128)}, bf16[256,6144]{1,0:T(8,128)(2,1)S(1)}, s32[]{:T(128)}, ...), condition=%wide.region_8.8_spmd, body=%wide.region_7.7_spmd.sunk | while | flops 3222667264 | bytes 79167672 | solution.py:92
  633.2 39.2 %all-to-all-done.2 = bf16[32,6,6144]{2,1,0:T(8,128)(2,1)S(1)} async-done(((bf16[32,6,6144]{2,1,0:T(8,128)(2,1)}), bf16[32,6,6144]{2,1,0:T(8,128)(2,1)S(1)}, u32[]{:S(2)}, u32[]{:S(2)}) %all-to-all-start.2) | async-done | bytes 2359328 | tf_op jit(solution)/shard_map/while/body/eval_jaxpr/all_to_all | solution.py:100
  732.0 15.5 all-to-all-done.1
  758.9 21.0 %while.50 = (s32[]{:T(128)}, bf16[256,6144]{1,0:T(8,128)(2,1)S(1)}, s32[]{:T(128)}, bf16[256,6144]{1,0:T(8,128)(2,1)}, bf16[6144,1024]{1,0:T(8,128)(2,1)}, /*ind...) while((s32[]{:T(128)}, bf16[256,6144]{1,0:T(8,128)(2,1)S(1)}, s32[]{:T(128)}, ...), condition=%wide.region_8.8_spmd, body=%wide.region_7.7_spmd.sunk | while | flops 3222667264 | bytes 79167672 | solution.py:92
  794.9 39.2 %all-to-all-done.2 = bf16[32,6,6144]{2,1,0:T(8,128)(2,1)S(1)} async-done(((bf16[32,6,6144]{2,1,0:T(8,128)(2,1)}), bf16[32,6,6144]{2,1,0:T(8,128)(2,1)S(1)}, u32[]{:S(2)}, u32[]{:S(2)}) %all-to-all-start.2) | async-done | bytes 2359328 | tf_op jit(solution)/shard_map/while/body/eval_jaxpr/all_to_all | solution.py:100
  893.7 15.5 all-to-all-done.1
  920.6 21.0 %while.50 = (s32[]{:T(128)}, bf16[256,6144]{1,0:T(8,128)(2,1)S(1)}, s32[]{:T(128)}, bf16[256,6144]{1,0:T(8,128)(2,1)}, bf16[6144,1024]{1,0:T(8,128)(2,1)}, /*ind...) while((s32[]{:T(128)}, bf16[256,6144]{1,0:T(8,128)(2,1)S(1)}, s32[]{:T(128)}, ...), condition=%wide.region_8.8_spmd, body=%wide.region_7.7_spmd.sunk | while | flops 3222667264 | bytes 79167672 | solution.py:92
  956.6 39.2 %all-to-all-done.2 = bf16[32,6,6144]{2,1,0:T(8,128)(2,1)S(1)} async-done(((bf16[32,6,6144]{2,1,0:T(8,128)(2,1)}), bf16[32,6,6144]{2,1,0:T(8,128)(2,1)S(1)}, u32[]{:S(2)}, u32[]{:S(2)}) %all-to-all-start.2) | async-done | bytes 2359328 | tf_op jit(solution)/shard_map/while/body/eval_jaxpr/all_to_all | solution.py:100
  1055.4 15.5 all-to-all-done.1
  1082.2 21.0 %while.50 = (s32[]{:T(128)}, bf16[256,6144]{1,0:T(8,128)(2,1)S(1)}, s32[]{:T(128)}, bf16[256,6144]{1,0:T(8,128)(2,1)}, bf16[6144,1024]{1,0:T(8,128)(2,1)}, /*ind...) while((s32[]{:T(128)}, bf16[256,6144]{1,0:T(8,128)(2,1)S(1)}, s32[]{:T(128)}, ...), condition=%wide.region_8.8_spmd, body=%wide.region_7.7_spmd.sunk | while | flops 3222667264 | bytes 79167672 | solution.py:92
  1118.3 39.2 %all-to-all-done.2 = bf16[32,6,6144]{2,1,0:T(8,128)(2,1)S(1)} async-done(((bf16[32,6,6144]{2,1,0:T(8,128)(2,1)}), bf16[32,6,6144]{2,1,0:T(8,128)(2,1)S(1)}, u32[]{:S(2)}, u32[]{:S(2)}) %all-to-all-start.2) | async-done | bytes 2359328 | tf_op jit(solution)/shard_map/while/body/eval_jaxpr/all_to_all | solution.py:100
  1243.9 21.0 %while.50 = (s32[]{:T(128)}, bf16[256,6144]{1,0:T(8,128)(2,1)S(1)}, s32[]{:T(128)}, bf16[256,6144]{1,0:T(8,128)(2,1)}, bf16[6144,1024]{1,0:T(8,128)(2,1)}, /*ind...) while((s32[]{:T(128)}, bf16[256,6144]{1,0:T(8,128)(2,1)S(1)}, s32[]{:T(128)}, ...), condition=%wide.region_8.8_spmd, body=%wide.region_7.7_spmd.sunk | while | flops 3222667264 | bytes 79167672 | solution.py:92
  1280.0 39.2 %all-to-all-done.2 = bf16[32,6,6144]{2,1,0:T(8,128)(2,1)S(1)} async-done(((bf16[32,6,6144]{2,1,0:T(8,128)(2,1)}), bf16[32,6,6144]{2,1,0:T(8,128)(2,1)S(1)}, u32[]{:S(2)}, u32[]{:S(2)}) %all-to-all-start.2) | async-done | bytes 2359328 | tf_op jit(solution)/shard_map/while/body/eval_jaxpr/all_to_all | solution.py:100
  1405.6 21.0 %while.50 = (s32[]{:T(128)}, bf16[256,6144]{1,0:T(8,128)(2,1)S(1)}, s32[]{:T(128)}, bf16[256,6144]{1,0:T(8,128)(2,1)}, bf16[6144,1024]{1,0:T(8,128)(2,1)}, /*ind...) while((s32[]{:T(128)}, bf16[256,6144]{1,0:T(8,128)(2,1)S(1)}, s32[]{:T(128)}, ...), condition=%wide.region_8.8_spmd, body=%wide.region_7.7_spmd.sunk | while | flops 3222667264 | bytes 79167672 | solution.py:92
  1441.7 39.2 %all-to-all-done.2 = bf16[32,6,6144]{2,1,0:T(8,128)(2,1)S(1)} async-done(((bf16[32,6,6144]{2,1,0:T(8,128)(2,1)}), bf16[32,6,6144]{2,1,0:T(8,128)(2,1)S(1)}, u32[]{:S(2)}, u32[]{:S(2)}) %all-to-all-start.2) | async-done | bytes 2359328 | tf_op jit(solution)/shard_map/while/body/eval_jaxpr/all_to_all | solution.py:100
  1540.4 15.5 all-to-all-done.1
  1567.3 21.0 %while.50 = (s32[]{:T(128)}, bf16[256,6144]{1,0:T(8,128)(2,1)S(1)}, s32[]{:T(128)}, bf16[256,6144]{1,0:T(8,128)(2,1)}, bf16[6144,1024]{1,0:T(8,128)(2,1)}, /*ind...) while((s32[]{:T(128)}, bf16[256,6144]{1,0:T(8,128)(2,1)S(1)}, s32[]{:T(128)}, ...), condition=%wide.region_8.8_spmd, body=%wide.region_7.7_spmd.sunk | while | flops 3222667264 | bytes 79167672 | solution.py:92
  1603.3 39.2 %all-to-all-done.2 = bf16[32,6,6144]{2,1,0:T(8,128)(2,1)S(1)} async-done(((bf16[32,6,6144]{2,1,0:T(8,128)(2,1)}), bf16[32,6,6144]{2,1,0:T(8,128)(2,1)S(1)}, u32[]{:S(2)}, u32[]{:S(2)}) %all-to-all-start.2) | async-done | bytes 2359328 | tf_op jit(solution)/shard_map/while/body/eval_jaxpr/all_to_all | solution.py:100
  1702.1 15.5 all-to-all-done.1
  1729.0 21.0 %while.50 = (s32[]{:T(128)}, bf16[256,6144]{1,0:T(8,128)(2,1)S(1)}, s32[]{:T(128)}, bf16[256,6144]{1,0:T(8,128)(2,1)}, bf16[6144,1024]{1,0:T(8,128)(2,1)}, /*ind...) while((s32[]{:T(128)}, bf16[256,6144]{1,0:T(8,128)(2,1)S(1)}, s32[]{:T(128)}, ...), condition=%wide.region_8.8_spmd, body=%wide.region_7.7_spmd.sunk | while | flops 3222667264 | bytes 79167672 | solution.py:92
  1765.0 39.2 %all-to-all-done.2 = bf16[32,6,6144]{2,1,0:T(8,128)(2,1)S(1)} async-done(((bf16[32,6,6144]{2,1,0:T(8,128)(2,1)}), bf16[32,6,6144]{2,1,0:T(8,128)(2,1)S(1)}, u32[]{:S(2)}, u32[]{:S(2)}) %all-to-all-start.2) | async-done | bytes 2359328 | tf_op jit(solution)/shard_map/while/body/eval_jaxpr/all_to_all | solution.py:100
  (745 shorter events, 1213.6 us)
Async XLA Ops:
  6.5 32.5 %all-gather.2.cloned.1.call-start = ((), (), s32[]{:S(2)}) async-start(), calls=%async_computation.3 | async-start | bytes 1966080 | tf_op jit(solution)/shard_map/all_gather | solution.py:31
  41.9 14.5 all-to-all-start
  58.5 44.4 %all-to-all-start.1 = ((bf16[32,6,6144]{2,1,0:T(8,128)(2,1)}), bf16[32,6,6144]{2,1,0:T(8,128)(2,1)}, u32[]{:S(2)}, u32[]{:S(2)}) async-start(bf16[32,6,6144]{2,1,0:T(8,128)(2,1)} %bitcast.140), calls=%async_computation.1 | async-start | bytes 6291456 | tf_op jit(solution)/shard_map/while/body/eval_jaxpr/all_to_all | solution.py:69
  143.6 45.8 %all-to-all-start.2 = ((bf16[32,6,6144]{2,1,0:T(8,128)(2,1)}), bf16[32,6,6144]{2,1,0:T(8,128)(2,1)S(1)}, u32[]{:S(2)}, u32[]{:S(2)}) async-start(bf16[32,6,6144]{2,1,0:T(8,128)(2,1)} %select_select_fusion.4), calls=%async_computation.2 | async-start | bytes 6291456 | tf_op jit(solution)/shard_map/while/body/eval_jaxpr/all_to_all | solution.py:100
  201.8 14.3 all-to-all-start
  218.1 44.4 %all-to-all-start.1 = ((bf16[32,6,6144]{2,1,0:T(8,128)(2,1)}), bf16[32,6,6144]{2,1,0:T(8,128)(2,1)}, u32[]{:S(2)}, u32[]{:S(2)}) async-start(bf16[32,6,6144]{2,1,0:T(8,128)(2,1)} %bitcast.140), calls=%async_computation.1 | async-start | bytes 6291456 | tf_op jit(solution)/shard_map/while/body/eval_jaxpr/all_to_all | solution.py:69
  303.2 45.8 %all-to-all-start.2 = ((bf16[32,6,6144]{2,1,0:T(8,128)(2,1)}), bf16[32,6,6144]{2,1,0:T(8,128)(2,1)S(1)}, u32[]{:S(2)}, u32[]{:S(2)}) async-start(bf16[32,6,6144]{2,1,0:T(8,128)(2,1)} %select_select_fusion.4), calls=%async_computation.2 | async-start | bytes 6291456 | tf_op jit(solution)/shard_map/while/body/eval_jaxpr/all_to_all | solution.py:100
  363.4 14.3 all-to-all-start
  379.8 44.4 %all-to-all-start.1 = ((bf16[32,6,6144]{2,1,0:T(8,128)(2,1)}), bf16[32,6,6144]{2,1,0:T(8,128)(2,1)}, u32[]{:S(2)}, u32[]{:S(2)}) async-start(bf16[32,6,6144]{2,1,0:T(8,128)(2,1)} %bitcast.140), calls=%async_computation.1 | async-start | bytes 6291456 | tf_op jit(solution)/shard_map/while/body/eval_jaxpr/all_to_all | solution.py:69
  464.9 45.8 %all-to-all-start.2 = ((bf16[32,6,6144]{2,1,0:T(8,128)(2,1)}), bf16[32,6,6144]{2,1,0:T(8,128)(2,1)S(1)}, u32[]{:S(2)}, u32[]{:S(2)}) async-start(bf16[32,6,6144]{2,1,0:T(8,128)(2,1)} %select_select_fusion.4), calls=%async_computation.2 | async-start | bytes 6291456 | tf_op jit(solution)/shard_map/while/body/eval_jaxpr/all_to_all | solution.py:100
  525.1 14.3 all-to-all-start
  541.5 44.4 %all-to-all-start.1 = ((bf16[32,6,6144]{2,1,0:T(8,128)(2,1)}), bf16[32,6,6144]{2,1,0:T(8,128)(2,1)}, u32[]{:S(2)}, u32[]{:S(2)}) async-start(bf16[32,6,6144]{2,1,0:T(8,128)(2,1)} %bitcast.140), calls=%async_computation.1 | async-start | bytes 6291456 | tf_op jit(solution)/shard_map/while/body/eval_jaxpr/all_to_all | solution.py:69
  626.6 45.8 %all-to-all-start.2 = ((bf16[32,6,6144]{2,1,0:T(8,128)(2,1)}), bf16[32,6,6144]{2,1,0:T(8,128)(2,1)S(1)}, u32[]{:S(2)}, u32[]{:S(2)}) async-start(bf16[32,6,6144]{2,1,0:T(8,128)(2,1)} %select_select_fusion.4), calls=%async_computation.2 | async-start | bytes 6291456 | tf_op jit(solution)/shard_map/while/body/eval_jaxpr/all_to_all | solution.py:100
  686.8 14.3 all-to-all-start
  703.1 44.4 %all-to-all-start.1 = ((bf16[32,6,6144]{2,1,0:T(8,128)(2,1)}), bf16[32,6,6144]{2,1,0:T(8,128)(2,1)}, u32[]{:S(2)}, u32[]{:S(2)}) async-start(bf16[32,6,6144]{2,1,0:T(8,128)(2,1)} %bitcast.140), calls=%async_computation.1 | async-start | bytes 6291456 | tf_op jit(solution)/shard_map/while/body/eval_jaxpr/all_to_all | solution.py:69
  788.3 45.8 %all-to-all-start.2 = ((bf16[32,6,6144]{2,1,0:T(8,128)(2,1)}), bf16[32,6,6144]{2,1,0:T(8,128)(2,1)S(1)}, u32[]{:S(2)}, u32[]{:S(2)}) async-start(bf16[32,6,6144]{2,1,0:T(8,128)(2,1)} %select_select_fusion.4), calls=%async_computation.2 | async-start | bytes 6291456 | tf_op jit(solution)/shard_map/while/body/eval_jaxpr/all_to_all | solution.py:100
  848.5 14.3 all-to-all-start
  864.8 44.4 %all-to-all-start.1 = ((bf16[32,6,6144]{2,1,0:T(8,128)(2,1)}), bf16[32,6,6144]{2,1,0:T(8,128)(2,1)}, u32[]{:S(2)}, u32[]{:S(2)}) async-start(bf16[32,6,6144]{2,1,0:T(8,128)(2,1)} %bitcast.140), calls=%async_computation.1 | async-start | bytes 6291456 | tf_op jit(solution)/shard_map/while/body/eval_jaxpr/all_to_all | solution.py:69
  950.0 45.8 %all-to-all-start.2 = ((bf16[32,6,6144]{2,1,0:T(8,128)(2,1)}), bf16[32,6,6144]{2,1,0:T(8,128)(2,1)S(1)}, u32[]{:S(2)}, u32[]{:S(2)}) async-start(bf16[32,6,6144]{2,1,0:T(8,128)(2,1)} %select_select_fusion.4), calls=%async_computation.2 | async-start | bytes 6291456 | tf_op jit(solution)/shard_map/while/body/eval_jaxpr/all_to_all | solution.py:100
  1010.2 14.3 all-to-all-start
  1026.5 44.4 %all-to-all-start.1 = ((bf16[32,6,6144]{2,1,0:T(8,128)(2,1)}), bf16[32,6,6144]{2,1,0:T(8,128)(2,1)}, u32[]{:S(2)}, u32[]{:S(2)}) async-start(bf16[32,6,6144]{2,1,0:T(8,128)(2,1)} %bitcast.140), calls=%async_computation.1 | async-start | bytes 6291456 | tf_op jit(solution)/shard_map/while/body/eval_jaxpr/all_to_all | solution.py:69
  1111.7 45.8 %all-to-all-start.2 = ((bf16[32,6,6144]{2,1,0:T(8,128)(2,1)}), bf16[32,6,6144]{2,1,0:T(8,128)(2,1)S(1)}, u32[]{:S(2)}, u32[]{:S(2)}) async-start(bf16[32,6,6144]{2,1,0:T(8,128)(2,1)} %select_select_fusion.4), calls=%async_computation.2 | async-start | bytes 6291456 | tf_op jit(solution)/shard_map/while/body/eval_jaxpr/all_to_all | solution.py:100
  1171.9 14.3 all-to-all-start
  1188.2 44.4 %all-to-all-start.1 = ((bf16[32,6,6144]{2,1,0:T(8,128)(2,1)}), bf16[32,6,6144]{2,1,0:T(8,128)(2,1)}, u32[]{:S(2)}, u32[]{:S(2)}) async-start(bf16[32,6,6144]{2,1,0:T(8,128)(2,1)} %bitcast.140), calls=%async_computation.1 | async-start | bytes 6291456 | tf_op jit(solution)/shard_map/while/body/eval_jaxpr/all_to_all | solution.py:69
  1273.3 45.8 %all-to-all-start.2 = ((bf16[32,6,6144]{2,1,0:T(8,128)(2,1)}), bf16[32,6,6144]{2,1,0:T(8,128)(2,1)S(1)}, u32[]{:S(2)}, u32[]{:S(2)}) async-start(bf16[32,6,6144]{2,1,0:T(8,128)(2,1)} %select_select_fusion.4), calls=%async_computation.2 | async-start | bytes 6291456 | tf_op jit(solution)/shard_map/while/body/eval_jaxpr/all_to_all | solution.py:100
  1333.5 14.3 all-to-all-start
  1349.9 44.4 %all-to-all-start.1 = ((bf16[32,6,6144]{2,1,0:T(8,128)(2,1)}), bf16[32,6,6144]{2,1,0:T(8,128)(2,1)}, u32[]{:S(2)}, u32[]{:S(2)}) async-start(bf16[32,6,6144]{2,1,0:T(8,128)(2,1)} %bitcast.140), calls=%async_computation.1 | async-start | bytes 6291456 | tf_op jit(solution)/shard_map/while/body/eval_jaxpr/all_to_all | solution.py:69
  1435.0 45.8 %all-to-all-start.2 = ((bf16[32,6,6144]{2,1,0:T(8,128)(2,1)}), bf16[32,6,6144]{2,1,0:T(8,128)(2,1)S(1)}, u32[]{:S(2)}, u32[]{:S(2)}) async-start(bf16[32,6,6144]{2,1,0:T(8,128)(2,1)} %select_select_fusion.4), calls=%async_computation.2 | async-start | bytes 6291456 | tf_op jit(solution)/shard_map/while/body/eval_jaxpr/all_to_all | solution.py:100
  1511.5 44.4 %all-to-all-start.1 = ((bf16[32,6,6144]{2,1,0:T(8,128)(2,1)}), bf16[32,6,6144]{2,1,0:T(8,128)(2,1)}, u32[]{:S(2)}, u32[]{:S(2)}) async-start(bf16[32,6,6144]{2,1,0:T(8,128)(2,1)} %bitcast.140), calls=%async_computation.1 | async-start | bytes 6291456 | tf_op jit(solution)/shard_map/while/body/eval_jaxpr/all_to_all | solution.py:69
  1596.7 45.8 %all-to-all-start.2 = ((bf16[32,6,6144]{2,1,0:T(8,128)(2,1)}), bf16[32,6,6144]{2,1,0:T(8,128)(2,1)S(1)}, u32[]{:S(2)}, u32[]{:S(2)}) async-start(bf16[32,6,6144]{2,1,0:T(8,128)(2,1)} %select_select_fusion.4), calls=%async_computation.2 | async-start | bytes 6291456 | tf_op jit(solution)/shard_map/while/body/eval_jaxpr/all_to_all | solution.py:100
  1673.2 44.4 %all-to-all-start.1 = ((bf16[32,6,6144]{2,1,0:T(8,128)(2,1)}), bf16[32,6,6144]{2,1,0:T(8,128)(2,1)}, u32[]{:S(2)}, u32[]{:S(2)}) async-start(bf16[32,6,6144]{2,1,0:T(8,128)(2,1)} %bitcast.140), calls=%async_computation.1 | async-start | bytes 6291456 | tf_op jit(solution)/shard_map/while/body/eval_jaxpr/all_to_all | solution.py:69
  1758.4 45.8 %all-to-all-start.2 = ((bf16[32,6,6144]{2,1,0:T(8,128)(2,1)}), bf16[32,6,6144]{2,1,0:T(8,128)(2,1)S(1)}, u32[]{:S(2)}, u32[]{:S(2)}) async-start(bf16[32,6,6144]{2,1,0:T(8,128)(2,1)} %select_select_fusion.4), calls=%async_computation.2 | async-start | bytes 6291456 | tf_op jit(solution)/shard_map/while/body/eval_jaxpr/all_to_all | solution.py:100
  (35 other events, 290.1 us)
Sparse Core Ops, SparseCore 0:
  9.0 29.9 all-gather.1
where the time goes:
time: 1840 us; the launch traced here: 1820 us
  waiting for transfers between devices  706 us (38%)
  other arithmetic  362 us (20%)
  local copies, waits for them, and re-layouts  273 us (15%)
  starting transfers between devices  251 us (14%)
  matrix products  207 us (11%)
    all_to_all x11, waiting for transfers between devices, section(): lax.all_to_all(returned, 'ed', split_axis=0, concat_axis=0, tiled=True)  431 us
    all_to_all x11, waiting for transfers between devices, section(): lax.all_to_all(outgoing.reshape(n_ed, most, width), 'ed', split_axis=0, c...  171 us
    and x11, other arithmetic, section(): compact = jnp.take(received, source_of * most + within, axis=0)  168 us
    dot_general x22, matrix products, expert_rows(): jnp.dot(rows, up_local, preferred_element_type=jnp.float32)  155 us
    all_to_all x11, starting transfers between devices, section(): lax.all_to_all(count_out, 'ed', split_axis=0, concat_axis=0, tiled=True)  79.7 us
    all_to_all x11, starting transfers between devices, section(): lax.all_to_all(returned, 'ed', split_axis=0, concat_axis=0, tiled=True)  72.3 us
    gather x22, local copies, waits for them, and re-layouts, section(): jnp.take(done, back_index.reshape(-1), axis=0).reshape(n_ed, most, width)  68.3 us
    all_to_all x11, starting transfers between devices, section(): lax.all_to_all(outgoing.reshape(n_ed, most, width), 'ed', split_axis=0, c...  55.4 us
  transfers between devices with their start and end apart: 45, of which 45 were waited for; matrix products, arithmetic and copies ran while one was open for 16% of the time, Pallas kernels for 0%

commit v1 on v0

v1 whole, which is shorter than its diff:
```python
import functools

import jax
import jax.numpy as jnp
from jax import lax
from jax.experimental import pallas as pl
from jax.experimental.pallas import tpu as pltpu
from jax.sharding import Mesh, PartitionSpec as P

EXPERTS = 4
MOST = 6
PAD = 8
STREAMS = 2
GATHER = False
LIMIT = 10
PERIOD = 75.0
OFFSET = 18.0
PHASES = (0.0, 10.0, 31.0, 40.0, 56.5, 66.0)
SECTIONS = 4
BF = jnp.bfloat16
F32 = jnp.float32


def dot(a, b):
    return jnp.dot(a, b, preferred_element_type=F32)


def whole(n):
    return [pl.BlockSpec(memory_space=pltpu.VMEM)] * n


def moved(value, axis, by):
    n = lax.axis_size(axis)
    return lax.ppermute(value, axis, [(i, (i + by) % n) for i in range(n)])


def stacked(refs):
    return jnp.concatenate([r[...].astype(F32) for r in refs], axis=0).astype(BF)


def joined(parts):
    return jnp.concatenate([p[0].astype(F32) for p in parts], axis=1)


def enter_kernel(step, source, idx, gain, table, *refs):
    ins, outs = refs[: len(refs) - 1 - EXPERTS], refs[len(refs) - 1 - EXPERTS :]
    if source == "inputs":
        values = joined(ins)
    elif source == "panel":
        values = ins[0][...].astype(F32)
    else:
        values = jnp.where(idx[step, 1] == 1, joined(ins[1:]), ins[0][...].astype(F32))
    outs[0][...] = values.astype(BF)
    scale = lax.rsqrt(jnp.mean(values * values, axis=-1, keepdims=True) + 1e-05)
    normed = (values * scale * gain[...]).astype(BF)
    packed = dot(table[idx[step, 0]], normed)
    for d in range(EXPERTS):
        outs[1 + d][...] = packed[d * PAD : (d + 1) * PAD].astype(BF)


def combine_kernel(step, idx, panel, hi, lo, b0, b1, b2, b3, produced):
    here = idx[step, 0]
    rows = stacked((b0, b1, b2, b3))
    mixed = dot(hi[here], rows) + dot(lo[here], rows)
    produced[...] = (panel[...].astype(F32) + mixed).astype(BF)


def tighten_kernel(b0, b1, b2, b3, out):
    rows = stacked((b0, b1, b2, b3))
    i = lax.broadcasted_iota(jnp.int32, (EXPERTS * MOST, EXPERTS * PAD), 0)
    j = lax.broadcasted_iota(jnp.int32, (EXPERTS * MOST, EXPERTS * PAD), 1)
    pick = (j == i + (i // MOST) * (PAD - MOST)).astype(F32).astype(BF)
    out[...] = dot(pick, rows).astype(BF)


def spread_kernel(own, r1, r2, r3, *outs):
    total = own[...].astype(F32) + r1[...].astype(F32) + r2[...].astype(F32) + r3[...].astype(F32)
    i = lax.broadcasted_iota(jnp.int32, (EXPERTS * PAD, EXPERTS * MOST), 0)
    j = lax.broadcasted_iota(jnp.int32, (EXPERTS * PAD, EXPERTS * MOST), 1)
    inside = (i % PAD) < MOST
    pick = ((i == j + (j // MOST) * (PAD - MOST)) & inside).astype(F32).astype(BF)
    blocks = dot(pick, total.astype(BF))
    for d, out in enumerate(outs):
        out[...] = blocks[d * PAD : (d + 1) * PAD].astype(BF)


def pair_kernel(own, other, *outs):
    n = outs[0].shape[0]
    for d, out in enumerate(outs):
        total = own[...].astype(F32)[d * n : (d + 1) * n] + other[...].astype(F32)[d * n : (d + 1) * n]
        out[...] = total.astype(BF)


def experts_kernel(order, *refs):
    rows, (up, down, keep, give, narrow, hid, wide) = refs[:-7], refs[-7:]
    width, units = up.shape
    n = keep.shape[0] // 4
    cols = wide.shape[1]
    if len(rows) == 8:
        for i in range(width // cols):
            at = pl.ds(i * cols, cols)
            for b in range(8):
                wide[b * n : (b + 1) * n, :] = rows[b][:, at].astype(F32)
            narrow[:, at] = wide[...].astype(BF)
        source = narrow
    else:
        source = rows[0]
    part = 256
    for i in range(units // part):
        at = pl.ds(i * part, part)
        v = dot(source[...], up[:, at])
        hid[:, at] = (v / (1.0 + jnp.exp(-v))).astype(BF)
    for i in range(width // cols):
        at = pl.ds(i * cols, cols)
        out = dot(hid[...], down[:, at])
        if len(rows) == 8:
            keep[:, at] = out[: 4 * n].astype(BF)
            give[:, at] = out[4 * n :].astype(BF)
        else:
            wide[...] = out
            for to, row in ((keep, 0), (give, 1)):
                picked = [wide[pl.ds(pl.multiple_of(order[row, d] * n, n), n), :] for d in range(4)]
                to[:, at] = jnp.concatenate(picked, axis=0).astype(BF)


SMEM = pl.BlockSpec(memory_space=pltpu.SMEM)


class Line:
    def call(self, kernel, outs, args, name, first=0, micro=None, scratch=(), limit=8, after=(), **extra):
        specs = [SMEM] * first + whole(len(args) - first)
        if micro is not None:
            specs[-4:] = [pl.BlockSpec((1, *a.shape[1:]), lambda i: (micro, 0, 0)) for a in args[-4:]]
            extra["grid"] = (1,)
        n_in, n_skip = len(args), len(after)

        def body(*refs):
            kernel(*refs[:n_in], *refs[n_in + n_skip :])

        return pl.pallas_call(
            body,
            out_shape=[jax.ShapeDtypeStruct(s, BF) for s in outs],
            in_specs=specs + [pl.BlockSpec(memory_space=pl.ANY)] * n_skip,
            out_specs=whole(len(outs)),
            scratch_shapes=list(scratch),
            compiler_params=pltpu.CompilerParams(vmem_limit_bytes=limit * 2**20),
            name=name,
            **extra,
        )(*args, *after)

    def experts(self, order, rows, up, down):
        width, units = up.shape
        n = sum(r.shape[0] for r in rows)
        return self.call(
            experts_kernel,
            [(n // 2, width)] * 2,
            [order, *rows, up, down],
            "experts",
            1,
            scratch=[
                pltpu.VMEM((n, width) if len(rows) > 1 else (16, 128), BF),
                pltpu.VMEM((n, units), BF),
                pltpu.VMEM((n, 768), F32),
            ],
            limit=LIMIT,
            cost_estimate=pl.CostEstimate(
                flops=4 * n * width * units, bytes_accessed=4 * n * width, transcendentals=n * units
            ),
        )


def slots_of(chosen, y):
    micro, tok, top = chosen.shape
    flat = chosen.reshape(micro, tok * top)
    order = jnp.arange(tok * top)
    same = (flat[:, :, None] == flat[:, None, :]) & (order[None, :, None] > order[None, None, :])
    rank = jnp.sum(same.astype(jnp.int32), axis=2).reshape(chosen.shape)
    distance = (chosen - y + EXPERTS) % EXPERTS
    return jnp.where(chosen < EXPERTS, distance * PAD + rank, -1)


def on_device(inputs, gain, w_up, w_down, routes, route_weight):
    micro, tok, _ = inputs.shape
    width = gain.shape[1]
    z, y, x, core = (lax.axis_index(a) for a in ("pipe", "y", "x", "core"))
    slots = EXPERTS * MOST
    block, column, panel_shape = (PAD, width), (slots, width), (tok, width)

    def gathered(part):
        return [part] + [lax.ppermute(part, "pipe", [(i, 0)]) for i in range(1, SECTIONS)]

    early, late = gathered(inputs[:STREAMS]), gathered(inputs[STREAMS:])

    def fresh(m):
        return (m, early) if m < STREAMS else (m - STREAMS, late)

    gain_row = gain.astype(F32)
    ids = jnp.arange(EXPERTS * PAD, dtype=jnp.int32)
    slot = slots_of(routes[0], y)
    table = jnp.any(slot[:, None, :, :] == ids[None, :, None, None], axis=3).astype(BF)
    weight = jnp.sum(jnp.where(slot[:, :, :, None] == ids, route_weight[0][:, :, :, None], 0.0), axis=2)
    hi = weight.astype(BF)
    lo = (weight - hi.astype(F32)).astype(BF)
    order = jnp.stack(
        [jnp.stack([2 * ((x - d) % 4) + (core + c) % 2 for d in range(4)]) for c in range(2)]
    ).astype(jnp.int32)

    def indices(stream, count):
        rows = []
        for t in range(count + SECTIONS - 1):
            m = stream + STREAMS * jnp.clip(t - z, 0, count - 1)
            place = jnp.where((t - z >= 0) & (t - z < count), m, micro)
            rows.append(jnp.stack([m, (z == 0).astype(m.dtype), place]))
        return jnp.stack(rows).astype(jnp.int32)

    counts = [len(range(a, micro, STREAMS)) for a in range(STREAMS)]
    idx = [indices(a, counts[a]) for a in range(STREAMS)]
    line = Line()
    result = [jnp.zeros((micro + 1, tok, width), BF)]
    state = [{} for _ in range(STREAMS)]

    x_busy = []

    def on_x():
        return x_busy[-1] if x_busy else []

    def enter(a, t, s):
        given = [idx[a], gain_row, table]
        m = None
        source = "panel"
        if t:
            given.append(s["from_before"])
        if t < counts[a]:
            m, parts = fresh(a + STREAMS * t)
            given += parts
            source = "either" if t else "inputs"
        s["panel"], *blocks = line.call(
            functools.partial(enter_kernel, t, source), [panel_shape] + [block] * 4, given, "enter", 1, m
        )
        s["rows"] = [blocks[0]] + [moved(blocks[d], "y", d) for d in range(1, 4)]

    def tighten(a, t, s):
        (own,) = line.call(tighten_kernel, [column], s["rows"], "tighten")
        if GATHER:
            s["all"] = [lax.all_gather(own, ("x", "core"), tiled=True)]
        else:
            mine = [own] + [moved(own, "x", d) for d in range(1, 4)]
            x_busy.append(mine[1:])
            s["all"] = mine + [moved(v, "core", 1) for v in mine]

    def experts(a, t, s):
        s["keep"], give = line.experts(order, s["all"], w_up[0], w_down[0])
        s["back"] = moved(give, "core", 1)

    def pair(a, t, s):
        sums = line.call(pair_kernel, [column] * 4, [s["keep"], s["back"]], "pair")
        s["home"] = [sums[0]] + [moved(sums[d], "x", -d) for d in range(1, 4)]
        x_busy.append(s["home"][1:])

    def spread(a, t, s):
        blocks = line.call(spread_kernel, [block] * 4, s["home"], "spread")
        s["arrived"] = [blocks[0]] + [moved(blocks[d], "y", -d) for d in range(1, 4)]

    def combine(a, t, s):
        (made,) = line.call(
            functools.partial(combine_kernel, t), [panel_shape], [idx[a], s["panel"], hi, lo, *s["arrived"]], "combine", 1
        )
        if t < counts[a] + SECTIONS - 2:
            s["from_before"] = lax.ppermute(made, "pipe", [(i, i + 1) for i in range(SECTIONS - 1)])
        result[0] = lax.dynamic_update_index_in_dim(result[0], made, idx[a][t, 2], 0)

    stages = (enter, tighten, experts, pair, spread, combine)
    plan = []
    for a in range(STREAMS):
        for t in range(counts[a] + SECTIONS - 1):
            for at, stage in zip(PHASES, stages):
                plan.append((t * PERIOD + a * OFFSET + at, a, t, stage))
    for _, a, t, stage in sorted(plan, key=lambda p: p[0]):
        stage(a, t, state[a])
    return result[0][None, :micro]


def solution(mesh):
    devices = mesh.devices
    wide = Mesh(devices.reshape(devices.shape[0], 4, 4, 2), ("pipe", "y", "x", "core"))
    ed = ("y", "x", "core")
    in_specs = (
        P(None, ed, "pipe"),
        P("pipe", None),
        P("pipe", None, ed),
        P("pipe", ed, None),
        P("pipe", None, ed, None),
        P("pipe", None, ed, None),
    )
    return jax.shard_map(
        on_device, mesh=wide, in_specs=in_specs, out_specs=P("pipe", None, ed, None), check_vma=False
    )
```

time: 1840 us -> 779 us (0.42)
  waiting for transfers between devices: 706 us -> 246 us
  other arithmetic: 362 us -> 2.69 us
  local copies, waits for them, and re-layouts: 273 us -> 56.3 us
  matrix products: 207 us -> 0 us
  Pallas kernels: 0 us -> 120 us
  starting transfers between devices: 251 us -> 318 us
    all_to_all x33 -> x0, waiting for transfers between devices: 647 us -> none  [the longest x11 431 us: section(): lax.all_to_all(returned, 'ed', split_axis=0, concat_axis=0, tiled=True)]
    ppermute x11 -> x256, starting transfers between devices: 43.1 us -> 318 us  [the longest x238 276 us: moved(): return lax.ppermute(value, axis, [(i, (i + by) % n) for i in range(n)])]
    ppermute x11 -> x256, waiting for transfers between devices: 28.4 us -> 246 us  [the longest x238 240 us: moved(): return lax.ppermute(value, axis, [(i, (i + by) % n) for i in range(n)])]
    all_to_all x33 -> x0, starting transfers between devices: 207 us -> none  [the longest x11 79.7 us: section(): lax.all_to_all(count_out, 'ed', split_axis=0, concat_axis=0, tiled=True)]
    dot_general x55 -> x0, matrix products: 207 us -> none  [the longest x22 155 us: expert_rows(): jnp.dot(rows, up_local, preferred_element_type=jnp.float32)]
    and x22 -> x0, other arithmetic: 168 us -> none  [the longest x11 168 us: section(): compact = jnp.take(received, source_of * most + within, axis=0)]
    gather x77 -> x0, local copies, waits for them, and re-layouts: 144 us -> none  [the longest x22 68.3 us: section(): jnp.take(done, back_index.reshape(-1), axis=0).reshape(n_ed, most, width)]
    pallas_call x0 -> x82, Pallas kernels: none -> 120 us  [call(): pl.pallas_call(body, out_shape=[jax.ShapeDtypeStruct(s, BF) for s in outs...]
  transfers between devices with their start and end apart: 45 -> 256, of which waited for: 45 -> 75; matrix products, arithmetic and copies ran while one was open for 16% -> 2% of each run, Pallas kernels for 0% -> 15%
where the time goes in v1:
time: 779 us; the launch traced here: 771 us
  starting transfers between devices  318 us (41%)
  waiting for transfers between devices  246 us (32%)
  Pallas kernels  120 us (15%)
  local copies, waits for them, and re-layouts  56.3 us (7%)
  between operations  28.2 us (4%)
    ppermute x238, starting transfers between devices, moved(): return lax.ppermute(value, axis, [(i, (i + by) % n) for i in range(n)])  276 us
    ppermute x238, waiting for transfers between devices, moved(): return lax.ppermute(value, axis, [(i, (i + by) % n) for i in range(n)])  240 us
    pallas_call x82, Pallas kernels, call(): pl.pallas_call(body, out_shape=[jax.ShapeDtypeStruct(s, BF) for s in outs...  120 us
    unnamed x99, local copies, waits for them, and re-layouts  43.1 us
    ppermute x12, starting transfers between devices, combine(): lax.ppermute(made, 'pipe', [(i, i + 1) for i in range(SECTIONS - 1)])  33.8 us
  transfers between devices with their start and end apart: 256, of which 75 were waited for; matrix products, arithmetic and copies ran while one was open for 2% of the time, Pallas kernels for 15%

profile of v1, /device:TPU:1, one launch (start us, length us, event | category | flops | bytes accessed | tf_op | source)
XLA Modules:
  0.0 771.1 jit_solution(10559545030039731205)
XLA Ops:
  75.6 6.8 experts.14
  89.6 6.4 experts.15
  108.3 7.5 collective-permute-done.16.refs_3_
  170.0 10.0 %collective-permute-start.48 = (bf16[24,6144]{1,0:T(8,128)(2,1)S(1)}, bf16[24,6144]{1,0:T(8,128)(2,1)S(1)}, u32[]{:S(2)}, u32[]{:S(2)}) collective-permute-start(bf16[24,6144]{1,0:T(8,128)(2,1)S(1)} %collective-permute-done.44.refs_2_), channel_id=1, source_target_pairs={{0,1},{1,0},{2,3},{3,2},{4,5},{5,4},{6,7},{7,6},{8,9},{9,8},{10,11... | collective-permute-start | bytes 884744 | tf_op jit(solution)/shard_map/ppermute | solution.py:34
  187.0 5.7 experts.16
  193.1 5.7 experts.17
  206.7 7.4 collective-permute-done.52.refs_1_
  264.6 6.0 collective-permute-done.82.refs_4_
  283.8 5.7 experts.18
  303.5 7.3 collective-permute-done.88.refs_1_
  316.9 7.0 collective-permute-done.106.refs_1_
  360.9 6.1 collective-permute-done.118.refs_4_
  373.2 5.7 collective-permute-start.122
  380.5 5.7 experts.20
  386.5 5.8 experts.21
  400.2 7.5 collective-permute-done.124.refs_1_
  413.8 6.8 collective-permute-done.142.refs_1_
  458.8 6.5 collective-permute-done.154.refs_4_
  478.4 5.7 experts.22
  484.5 5.8 experts.23
  497.9 7.2 collective-permute-done.160.refs_1_
  511.6 6.7 collective-permute-done.178.refs_1_
  620.1 6.5 experts.24
  626.8 6.4 experts.25
  644.6 7.0 collective-permute-done.198.refs_3_
  657.2 6.6 collective-permute-done.216.refs_3_
  696.5 6.1 collective-permute-done.226.refs_4_
  708.2 6.5 collective-permute-start.230
  716.2 5.7 experts.26
  722.2 5.8 experts.27
  740.7 6.5 collective-permute-done.234.refs_3_
  753.4 6.5 collective-permute-done.252.refs_3_
  (718 shorter events, 533.9 us)
Async XLA Ops:
  52.7 30.2 %collective-permute-start.26 = (bf16[24,6144]{1,0:T(8,128)(2,1)}, bf16[24,6144]{1,0:T(8,128)(2,1)S(1)}, u32[]{:S(2)}, u32[]{:S(2)}) collective-permute-start(bf16[24,6144]{1,0:T(8,128)(2,1)} %tighten.15.refs_1_), channel_id=1, source_target_pairs={{0,1},{1,0},{2,3},{3,2},{4,5},{5,4},{6,7},{7,6},{8,9},{9,8},{10,11... | collective-permute-start | bytes 884744 | tf_op jit(solution)/shard_map/ppermute | solution.py:34
  55.5 28.1 %collective-permute-start.27 = (bf16[24,6144]{1,0:T(8,128)(2,1)}, bf16[24,6144]{1,0:T(8,128)(2,1)S(1)}, u32[]{:S(2)}, u32[]{:S(2)}) collective-permute-start(bf16[24,6144]{1,0:T(8,128)(2,1)} %collective-permute-done.23.refs_2_), channel_id=1, source_target_pairs={{0,1},{1,0},{2,3},{3,2},{4,5},{5,4},{6,7},{7,6},{8,9},{9,8},{10,11... | collective-permute-start | bytes 884744 | tf_op jit(solution)/shard_map/ppermute | solution.py:34
  56.3 28.1 %collective-permute-start.28 = (bf16[24,6144]{1,0:T(8,128)(2,1)}, bf16[24,6144]{1,0:T(8,128)(2,1)S(1)}, u32[]{:S(2)}, u32[]{:S(2)}) collective-permute-start(bf16[24,6144]{1,0:T(8,128)(2,1)} %collective-permute-done.24.refs_3_), channel_id=1, source_target_pairs={{0,1},{1,0},{2,3},{3,2},{4,5},{5,4},{6,7},{7,6},{8,9},{9,8},{10,11... | collective-permute-start | bytes 884744 | tf_op jit(solution)/shard_map/ppermute | solution.py:34
  57.5 27.6 %collective-permute-start.29 = (bf16[24,6144]{1,0:T(8,128)(2,1)}, bf16[24,6144]{1,0:T(8,128)(2,1)S(1)}, u32[]{:S(2)}, u32[]{:S(2)}) collective-permute-start(bf16[24,6144]{1,0:T(8,128)(2,1)} %collective-permute-done.25.refs_4_), channel_id=1, source_target_pairs={{0,1},{1,0},{2,3},{3,2},{4,5},{5,4},{6,7},{7,6},{8,9},{9,8},{10,11... | collective-permute-start | bytes 884744 | tf_op jit(solution)/shard_map/ppermute | solution.py:34
  102.4 18.6 %collective-permute-start.32 = (bf16[24,6144]{1,0:T(8,128)(2,1)S(1)}, bf16[24,6144]{1,0:T(8,128)(2,1)S(1)}, u32[]{:S(2)}, u32[]{:S(2)}) collective-permute-start(bf16[24,6144]{1,0:T(8,128)(2,1)S(1)} %get-tuple-element.239), channel_id=1, source_target_pairs={{0,4},{2,6},{4,0},{6,2},{1,5},{3,7},{5,1},{7,3},{8,12},{10,14},{12... | collective-permute-start | bytes 884744 | tf_op jit(solution)/shard_map/ppermute | solution.py:34
  105.7 22.1 %collective-permute-start.33 = (bf16[24,6144]{1,0:T(8,128)(2,1)S(1)}, bf16[24,6144]{1,0:T(8,128)(2,1)S(1)}, u32[]{:S(2)}, u32[]{:S(2)}) collective-permute-start(bf16[24,6144]{1,0:T(8,128)(2,1)S(1)} %get-tuple-element.240), channel_id=1, source_target_pairs={{0,2},{2,4},{4,6},{6,0},{1,3},{3,5},{5,7},{7,1},{8,10},{10,12},{12... | collective-permute-start | bytes 884744 | tf_op jit(solution)/shard_map/ppermute | solution.py:34
  121.0 23.0 %collective-permute-start.38 = (bf16[6,16,1536]{2,1,0:T(8,128)(2,1)S(1)}, bf16[6,16,1536]{2,1,0:T(8,128)(2,1)S(1)}, u32[]{:S(2)}, u32[]{:S(2)}) collective-permute-start(bf16[6,16,1536]{2,1,0:T(8,128)(2,1)S(1)} %slice.54.refs_4_), channel_id=1, source_target_pairs={{32,0},{33,1},{34,2},{35,3},{36,4},{37,5},{38,6},{39,7},{40,8},{41... | collective-permute-start | bytes 884744 | tf_op jit(solution)/shard_map/ppermute | solution.py:190
  160.2 19.8 %collective-permute-start.47 = (bf16[24,6144]{1,0:T(8,128)(2,1)S(1)}, bf16[24,6144]{1,0:T(8,128)(2,1)S(1)}, u32[]{:S(2)}, u32[]{:S(2)}) collective-permute-start(bf16[24,6144]{1,0:T(8,128)(2,1)S(1)} %tighten.16.refs_1_), channel_id=1, source_target_pairs={{0,1},{1,0},{2,3},{3,2},{4,5},{5,4},{6,7},{7,6},{8,9},{9,8},{10,11... | collective-permute-start | bytes 884744 | tf_op jit(solution)/shard_map/ppermute | solution.py:34
  202.9 24.2 %collective-permute-start.70 = (bf16[24,6144]{1,0:T(8,128)(2,1)S(1)}, bf16[24,6144]{1,0:T(8,128)(2,1)S(1)}, u32[]{:S(2)}, u32[]{:S(2)}) collective-permute-start(bf16[24,6144]{1,0:T(8,128)(2,1)S(1)} %get-tuple-element.268), channel_id=1, source_target_pairs={{0,6},{2,0},{4,2},{6,4},{1,7},{3,1},{5,3},{7,5},{8,14},{10,8},{12,... | collective-permute-start | bytes 884744 | tf_op jit(solution)/shard_map/ppermute | solution.py:34
  204.9 23.5 %collective-permute-start.71 = (bf16[24,6144]{1,0:T(8,128)(2,1)S(1)}, bf16[24,6144]{1,0:T(8,128)(2,1)S(1)}, u32[]{:S(2)}, u32[]{:S(2)}) collective-permute-start(bf16[24,6144]{1,0:T(8,128)(2,1)S(1)} %get-tuple-element.269), channel_id=1, source_target_pairs={{0,4},{2,6},{4,0},{6,2},{1,5},{3,7},{5,1},{7,3},{8,12},{10,14},{12... | collective-permute-start | bytes 884744 | tf_op jit(solution)/shard_map/ppermute | solution.py:34
  255.9 18.5 %collective-permute-start.83 = (bf16[24,6144]{1,0:T(8,128)(2,1)S(1)}, bf16[24,6144]{1,0:T(8,128)(2,1)S(1)}, u32[]{:S(2)}, u32[]{:S(2)}) collective-permute-start(bf16[24,6144]{1,0:T(8,128)(2,1)S(1)} %tighten.18.refs_1_), channel_id=1, source_target_pairs={{0,1},{1,0},{2,3},{3,2},{4,5},{5,4},{6,7},{7,6},{8,9},{9,8},{10,11... | collective-permute-start | bytes 884744 | tf_op jit(solution)/shard_map/ppermute | solution.py:34
  299.6 24.2 %collective-permute-start.106 = (bf16[24,6144]{1,0:T(8,128)(2,1)S(1)}, bf16[24,6144]{1,0:T(8,128)(2,1)S(1)}, u32[]{:S(2)}, u32[]{:S(2)}) collective-permute-start(bf16[24,6144]{1,0:T(8,128)(2,1)S(1)} %get-tuple-element.298), channel_id=1, source_target_pairs={{0,6},{2,0},{4,2},{6,4},{1,7},{3,1},{5,3},{7,5},{8,14},{10,8},{12,... | collective-permute-start | bytes 884744 | tf_op jit(solution)/shard_map/ppermute | solution.py:34
  301.7 22.1 %collective-permute-start.107 = (bf16[24,6144]{1,0:T(8,128)(2,1)S(1)}, bf16[24,6144]{1,0:T(8,128)(2,1)S(1)}, u32[]{:S(2)}, u32[]{:S(2)}) collective-permute-start(bf16[24,6144]{1,0:T(8,128)(2,1)S(1)} %get-tuple-element.299), channel_id=1, source_target_pairs={{0,4},{2,6},{4,0},{6,2},{1,5},{3,7},{5,1},{7,3},{8,12},{10,14},{12... | collective-permute-start | bytes 884744 | tf_op jit(solution)/shard_map/ppermute | solution.py:34
  360.4 18.6 %collective-permute-start.135 = (bf16[24,6144]{1,0:T(8,128)(2,1)S(1)}, bf16[24,6144]{1,0:T(8,128)(2,1)S(1)}, u32[]{:S(2)}, u32[]{:S(2)}) collective-permute-start(bf16[24,6144]{1,0:T(8,128)(2,1)S(1)} %tighten.21.refs_1_), channel_id=1, source_target_pairs={{0,4},{2,6},{4,0},{6,2},{1,5},{3,7},{5,1},{7,3},{8,12},{10,14},{12... | collective-permute-start | bytes 884744 | tf_op jit(solution)/shard_map/ppermute | solution.py:34
  360.4 18.6 %collective-permute-start.136 = (bf16[24,6144]{1,0:T(8,128)(2,1)S(1)}, bf16[24,6144]{1,0:T(8,128)(2,1)S(1)}, u32[]{:S(2)}, u32[]{:S(2)}) collective-permute-start(bf16[24,6144]{1,0:T(8,128)(2,1)S(1)} %tighten.21.refs_1_), channel_id=1, source_target_pairs={{0,6},{2,0},{4,2},{6,4},{1,7},{3,1},{5,3},{7,5},{8,14},{10,8},{12,... | collective-permute-start | bytes 884744 | tf_op jit(solution)/shard_map/ppermute | solution.py:34
  396.4 24.2 %collective-permute-start.142 = (bf16[24,6144]{1,0:T(8,128)(2,1)S(1)}, bf16[24,6144]{1,0:T(8,128)(2,1)S(1)}, u32[]{:S(2)}, u32[]{:S(2)}) collective-permute-start(bf16[24,6144]{1,0:T(8,128)(2,1)S(1)} %get-tuple-element.328), channel_id=1, source_target_pairs={{0,6},{2,0},{4,2},{6,4},{1,7},{3,1},{5,3},{7,5},{8,14},{10,8},{12,... | collective-permute-start | bytes 884744 | tf_op jit(solution)/shard_map/ppermute | solution.py:34
  398.5 22.1 %collective-permute-start.143 = (bf16[24,6144]{1,0:T(8,128)(2,1)S(1)}, bf16[24,6144]{1,0:T(8,128)(2,1)S(1)}, u32[]{:S(2)}, u32[]{:S(2)}) collective-permute-start(bf16[24,6144]{1,0:T(8,128)(2,1)S(1)} %get-tuple-element.329), channel_id=1, source_target_pairs={{0,4},{2,6},{4,0},{6,2},{1,5},{3,7},{5,1},{7,3},{8,12},{10,14},{12... | collective-permute-start | bytes 884744 | tf_op jit(solution)/shard_map/ppermute | solution.py:34
  494.1 24.2 %collective-permute-start.178 = (bf16[24,6144]{1,0:T(8,128)(2,1)S(1)}, bf16[24,6144]{1,0:T(8,128)(2,1)S(1)}, u32[]{:S(2)}, u32[]{:S(2)}) collective-permute-start(bf16[24,6144]{1,0:T(8,128)(2,1)S(1)} %get-tuple-element.358), channel_id=1, source_target_pairs={{0,6},{2,0},{4,2},{6,4},{1,7},{3,1},{5,3},{7,5},{8,14},{10,8},{12,... | collective-permute-start | bytes 884744 | tf_op jit(solution)/shard_map/ppermute | solution.py:34
  496.2 22.1 %collective-permute-start.179 = (bf16[24,6144]{1,0:T(8,128)(2,1)S(1)}, bf16[24,6144]{1,0:T(8,128)(2,1)S(1)}, u32[]{:S(2)}, u32[]{:S(2)}) collective-permute-start(bf16[24,6144]{1,0:T(8,128)(2,1)S(1)} %get-tuple-element.359), channel_id=1, source_target_pairs={{0,4},{2,6},{4,0},{6,2},{1,5},{3,7},{5,1},{7,3},{8,12},{10,14},{12... | collective-permute-start | bytes 884744 | tf_op jit(solution)/shard_map/ppermute | solution.py:34
  547.3 19.0 %collective-permute-start.191 = (bf16[24,6144]{1,0:T(8,128)(2,1)S(1)}, bf16[24,6144]{1,0:T(8,128)(2,1)S(1)}, u32[]{:S(2)}, u32[]{:S(2)}) collective-permute-start(bf16[24,6144]{1,0:T(8,128)(2,1)S(1)} %tighten.24.refs_1_), channel_id=1, source_target_pairs={{0,1},{1,0},{2,3},{3,2},{4,5},{5,4},{6,7},{7,6},{8,9},{9,8},{10,11... | collective-permute-start | bytes 884744 | tf_op jit(solution)/shard_map/ppermute | solution.py:34
  555.8 52.9 %collective-permute-start.207 = (bf16[24,6144]{1,0:T(8,128)(2,1)S(1)}, bf16[24,6144]{1,0:T(8,128)(2,1)}, u32[]{:S(2)}, u32[]{:S(2)}) collective-permute-start(bf16[24,6144]{1,0:T(8,128)(2,1)S(1)} %tighten.25.refs_1_), channel_id=1, source_target_pairs={{0,4},{2,6},{4,0},{6,2},{1,5},{3,7},{5,1},{7,3},{8,12},{10,14},{12... | collective-permute-start | bytes 884744 | tf_op jit(solution)/shard_map/ppermute | solution.py:34
  555.9 53.0 %collective-permute-start.208 = (bf16[24,6144]{1,0:T(8,128)(2,1)S(1)}, bf16[24,6144]{1,0:T(8,128)(2,1)}, u32[]{:S(2)}, u32[]{:S(2)}) collective-permute-start(bf16[24,6144]{1,0:T(8,128)(2,1)S(1)} %tighten.25.refs_1_), channel_id=1, source_target_pairs={{0,6},{2,0},{4,2},{6,4},{1,7},{3,1},{5,3},{7,5},{8,14},{10,8},{12,... | collective-permute-start | bytes 884744 | tf_op jit(solution)/shard_map/ppermute | solution.py:34
  561.7 47.6 %collective-permute-start.192 = (bf16[24,6144]{1,0:T(8,128)(2,1)S(1)}, bf16[24,6144]{1,0:T(8,128)(2,1)}, u32[]{:S(2)}, u32[]{:S(2)}) collective-permute-start(bf16[24,6144]{1,0:T(8,128)(2,1)S(1)} %collective-permute-done.188.refs_2_), channel_id=1, source_target_pairs={{0,1},{1,0},{2,3},{3,2},{4,5},{5,4},{6,7},{7,6},{8,9},{9,8},{10,11... | collective-permute-start | bytes 884744 | tf_op jit(solution)/shard_map/ppermute | solution.py:34
  567.0 42.5 %collective-permute-start.193 = (bf16[24,6144]{1,0:T(8,128)(2,1)S(1)}, bf16[24,6144]{1,0:T(8,128)(2,1)}, u32[]{:S(2)}, u32[]{:S(2)}) collective-permute-start(bf16[24,6144]{1,0:T(8,128)(2,1)S(1)} %collective-permute-done.189.refs_3_), channel_id=1, source_target_pairs={{0,1},{1,0},{2,3},{3,2},{4,5},{5,4},{6,7},{7,6},{8,9},{9,8},{10,11... | collective-permute-start | bytes 884744 | tf_op jit(solution)/shard_map/ppermute | solution.py:34
  568.5 41.5 %collective-permute-start.194 = (bf16[24,6144]{1,0:T(8,128)(2,1)}, bf16[24,6144]{1,0:T(8,128)(2,1)}, u32[]{:S(2)}, u32[]{:S(2)}) collective-permute-start(bf16[24,6144]{1,0:T(8,128)(2,1)} %collective-permute-done.190.refs_4_), channel_id=1, source_target_pairs={{0,1},{1,0},{2,3},{3,2},{4,5},{5,4},{6,7},{7,6},{8,9},{9,8},{10,11... | collective-permute-start | bytes 884744 | tf_op jit(solution)/shard_map/ppermute | solution.py:34
  636.5 19.1 %collective-permute-start.214 = (bf16[24,6144]{1,0:T(8,128)(2,1)S(1)}, bf16[24,6144]{1,0:T(8,128)(2,1)S(1)}, u32[]{:S(2)}, u32[]{:S(2)}) collective-permute-start(bf16[24,6144]{1,0:T(8,128)(2,1)S(1)} %get-tuple-element.388), channel_id=1, source_target_pairs={{0,6},{2,0},{4,2},{6,4},{1,7},{3,1},{5,3},{7,5},{8,14},{10,8},{12,... | collective-permute-start | bytes 884744 | tf_op jit(solution)/shard_map/ppermute | solution.py:34
  638.6 18.6 %collective-permute-start.215 = (bf16[24,6144]{1,0:T(8,128)(2,1)S(1)}, bf16[24,6144]{1,0:T(8,128)(2,1)S(1)}, u32[]{:S(2)}, u32[]{:S(2)}) collective-permute-start(bf16[24,6144]{1,0:T(8,128)(2,1)S(1)} %get-tuple-element.389), channel_id=1, source_target_pairs={{0,4},{2,6},{4,0},{6,2},{1,5},{3,7},{5,1},{7,3},{8,12},{10,14},{12... | collective-permute-start | bytes 884744 | tf_op jit(solution)/shard_map/ppermute | solution.py:34
  642.9 21.0 %collective-permute-start.216 = (bf16[24,6144]{1,0:T(8,128)(2,1)S(1)}, bf16[24,6144]{1,0:T(8,128)(2,1)S(1)}, u32[]{:S(2)}, u32[]{:S(2)}) collective-permute-start(bf16[24,6144]{1,0:T(8,128)(2,1)S(1)} %get-tuple-element.390), channel_id=1, source_target_pairs={{0,2},{2,4},{4,6},{6,0},{1,3},{3,5},{5,7},{7,1},{8,10},{10,12},{12... | collective-permute-start | bytes 884744 | tf_op jit(solution)/shard_map/ppermute | solution.py:34
  687.7 18.5 %collective-permute-start.227 = (bf16[24,6144]{1,0:T(8,128)(2,1)S(1)}, bf16[24,6144]{1,0:T(8,128)(2,1)S(1)}, u32[]{:S(2)}, u32[]{:S(2)}) collective-permute-start(bf16[24,6144]{1,0:T(8,128)(2,1)S(1)} %tighten.26.refs_1_), channel_id=1, source_target_pairs={{0,1},{1,0},{2,3},{3,2},{4,5},{5,4},{6,7},{7,6},{8,9},{9,8},{10,11... | collective-permute-start | bytes 884744 | tf_op jit(solution)/shard_map/ppermute | solution.py:34
  695.1 19.6 %collective-permute-start.243 = (bf16[24,6144]{1,0:T(8,128)(2,1)S(1)}, bf16[24,6144]{1,0:T(8,128)(2,1)S(1)}, u32[]{:S(2)}, u32[]{:S(2)}) collective-permute-start(bf16[24,6144]{1,0:T(8,128)(2,1)S(1)} %tighten.27.refs_1_), channel_id=1, source_target_pairs={{0,4},{2,6},{4,0},{6,2},{1,5},{3,7},{5,1},{7,3},{8,12},{10,14},{12... | collective-permute-start | bytes 884744 | tf_op jit(solution)/shard_map/ppermute | solution.py:34
  734.0 19.4 %collective-permute-start.251 = (bf16[24,6144]{1,0:T(8,128)(2,1)S(1)}, bf16[24,6144]{1,0:T(8,128)(2,1)S(1)}, u32[]{:S(2)}, u32[]{:S(2)}) collective-permute-start(bf16[24,6144]{1,0:T(8,128)(2,1)S(1)} %get-tuple-element.419), channel_id=1, source_target_pairs={{0,4},{2,6},{4,0},{6,2},{1,5},{3,7},{5,1},{7,3},{8,12},{10,14},{12... | collective-permute-start | bytes 884744 | tf_op jit(solution)/shard_map/ppermute | solution.py:34
  737.6 22.3 %collective-permute-start.252 = (bf16[24,6144]{1,0:T(8,128)(2,1)S(1)}, bf16[24,6144]{1,0:T(8,128)(2,1)S(1)}, u32[]{:S(2)}, u32[]{:S(2)}) collective-permute-start(bf16[24,6144]{1,0:T(8,128)(2,1)S(1)} %get-tuple-element.420), channel_id=1, source_target_pairs={{0,2},{2,4},{4,6},{6,0},{1,3},{3,5},{5,7},{7,1},{8,10},{10,12},{12... | collective-permute-start | bytes 884744 | tf_op jit(solution)/shard_map/ppermute | solution.py:34
  (273 other events, 2877.0 us)

commit v2 on v1

--- a/solution.py
+++ b/solution.py
@@ -11,11 +11,7 @@
 MOST = 6
 PAD = 8
 STREAMS = 2
-GATHER = False
-LIMIT = 10
-PERIOD = 75.0
-OFFSET = 18.0
-PHASES = (0.0, 10.0, 31.0, 40.0, 56.5, 66.0)
+COST = 1
 SECTIONS = 4
 BF = jnp.bfloat16
 F32 = jnp.float32
@@ -91,81 +87,69 @@
         out[...] = total.astype(BF)
 
 
-def experts_kernel(order, *refs):
-    rows, (up, down, keep, give, narrow, hid, wide) = refs[:-7], refs[-7:]
+def stack_kernel(own, r1, r2, r3, out):
+    out[...] = stacked((own, r1, r2, r3))
+
+
+def experts_kernel(mine, theirs, up, down, keep, give, hid):
     width, units = up.shape
-    n = keep.shape[0] // 4
-    cols = wide.shape[1]
-    if len(rows) == 8:
-        for i in range(width // cols):
-            at = pl.ds(i * cols, cols)
-            for b in range(8):
-                wide[b * n : (b + 1) * n, :] = rows[b][:, at].astype(F32)
-            narrow[:, at] = wide[...].astype(BF)
-        source = narrow
-    else:
-        source = rows[0]
+    half = mine.shape[0]
+    rows = jnp.concatenate([mine[...], theirs[...]], axis=0)
     part = 256
     for i in range(units // part):
         at = pl.ds(i * part, part)
-        v = dot(source[...], up[:, at])
+        v = dot(rows, up[:, at])
         hid[:, at] = (v / (1.0 + jnp.exp(-v))).astype(BF)
-    for i in range(width // cols):
-        at = pl.ds(i * cols, cols)
+    part = 768
+    for i in range(width // part):
+        at = pl.ds(i * part, part)
         out = dot(hid[...], down[:, at])
-        if len(rows) == 8:
-            keep[:, at] = out[: 4 * n].astype(BF)
-            give[:, at] = out[4 * n :].astype(BF)
-        else:
-            wide[...] = out
-            for to, row in ((keep, 0), (give, 1)):
-                picked = [wide[pl.ds(pl.multiple_of(order[row, d] * n, n), n), :] for d in range(4)]
-                to[:, at] = jnp.concatenate(picked, axis=0).astype(BF)
+        keep[:, at] = out[:half].astype(BF)
+        give[:, at] = out[half:].astype(BF)
 
 
 SMEM = pl.BlockSpec(memory_space=pltpu.SMEM)
 
 
 class Line:
-    def call(self, kernel, outs, args, name, first=0, micro=None, scratch=(), limit=8, after=(), **extra):
+    def __init__(self):
+        self.token = jnp.zeros((8, 128), F32)
+
+    def call(self, kernel, outs, args, name, first=0, micro=None, scratch=(), limit=6, **extra):
         specs = [SMEM] * first + whole(len(args) - first)
         if micro is not None:
             specs[-4:] = [pl.BlockSpec((1, *a.shape[1:]), lambda i: (micro, 0, 0)) for a in args[-4:]]
             extra["grid"] = (1,)
-        n_in, n_skip = len(args), len(after)
+        n_in, n_out = len(args), len(outs)
 
         def body(*refs):
-            kernel(*refs[:n_in], *refs[n_in + n_skip :])
-
-        return pl.pallas_call(
+            before, after = refs[n_in], refs[n_in + 1 + n_out]
+            kernel(*refs[:n_in], *refs[n_in + 1 : n_in + 1 + n_out], *refs[n_in + 2 + n_out :])
+            after[...] = before[...]
+
+        *result, self.token = pl.pallas_call(
             body,
-            out_shape=[jax.ShapeDtypeStruct(s, BF) for s in outs],
-            in_specs=specs + [pl.BlockSpec(memory_space=pl.ANY)] * n_skip,
-            out_specs=whole(len(outs)),
+            out_shape=[jax.ShapeDtypeStruct(s, BF) for s in outs] + [jax.ShapeDtypeStruct((8, 128), F32)],
+            in_specs=specs + whole(1),
+            out_specs=whole(n_out + 1),
             scratch_shapes=list(scratch),
             compiler_params=pltpu.CompilerParams(vmem_limit_bytes=limit * 2**20),
+            cost_estimate=pl.CostEstimate(flops=COST, bytes_accessed=COST, transcendentals=0),
             name=name,
             **extra,
-        )(*args, *after)
-
-    def experts(self, order, rows, up, down):
+        )(*args, self.token)
+        return result
+
+    def experts(self, rows, up, down):
         width, units = up.shape
-        n = sum(r.shape[0] for r in rows)
+        half = rows[0].shape[0]
         return self.call(
             experts_kernel,
-            [(n // 2, width)] * 2,
-            [order, *rows, up, down],
+            [(half, width)] * 2,
+            [*rows, up, down],
             "experts",
-            1,
-            scratch=[
-                pltpu.VMEM((n, width) if len(rows) > 1 else (16, 128), BF),
-                pltpu.VMEM((n, units), BF),
-                pltpu.VMEM((n, 768), F32),
-            ],
-            limit=LIMIT,
-            cost_estimate=pl.CostEstimate(
-                flops=4 * n * width * units, bytes_accessed=4 * n * width, transcendentals=n * units
-            ),
+            scratch=[pltpu.VMEM((2 * half, units), BF)],
+            limit=10,
         )
 
 
@@ -179,10 +163,37 @@
     return jnp.where(chosen < EXPERTS, distance * PAD + rank, -1)
 
 
+STAGES = (
+    (1.0, 3.5, "y", 4.0, 3.5),
+    (0.3, 4.0, "x", 11.8, 2.5),
+    (0.5, 0.3, "core", 2.0, 0.8),
+    (5.9, 0.3, "core", 2.0, 0.8),
+    (0.4, 4.0, "x", 11.8, 2.5),
+    (0.3, 3.5, "y", 4.0, 3.5),
+    (0.9, 1.5, "pipe", 4.0, 4.0),
+)
+
+
+def planned(totals):
+    done, ready, links = [0] * len(totals), [0.0] * len(totals), {}
+    now, order = 0.0, []
+    while len(order) < sum(totals):
+        left = [a for a in range(len(totals)) if done[a] < totals[a]]
+        a = min(left, key=lambda a: (max(now, ready[a]), done[a] - totals[a]))
+        kernel, starts, link, busy, latency = STAGES[done[a] % len(STAGES)]
+        now = max(now, ready[a]) + kernel
+        links[link] = max(now + 0.4 * starts, links.get(link, 0.0)) + busy
+        ready[a] = max(links[link] + latency, now + starts)
+        now += starts
+        done[a] += 1
+        order.append(a)
+    return order
+
+
 def on_device(inputs, gain, w_up, w_down, routes, route_weight):
     micro, tok, _ = inputs.shape
     width = gain.shape[1]
-    z, y, x, core = (lax.axis_index(a) for a in ("pipe", "y", "x", "core"))
+    z, y = lax.axis_index("pipe"), lax.axis_index("y")
     slots = EXPERTS * MOST
     block, column, panel_shape = (PAD, width), (slots, width), (tok, width)
 
@@ -201,28 +212,22 @@
     weight = jnp.sum(jnp.where(slot[:, :, :, None] == ids, route_weight[0][:, :, :, None], 0.0), axis=2)
     hi = weight.astype(BF)
     lo = (weight - hi.astype(F32)).astype(BF)
-    order = jnp.stack(
-        [jnp.stack([2 * ((x - d) % 4) + (core + c) % 2 for d in range(4)]) for c in range(2)]
-    ).astype(jnp.int32)
-
     def indices(stream, count):
         rows = []
         for t in range(count + SECTIONS - 1):
             m = stream + STREAMS * jnp.clip(t - z, 0, count - 1)
-            place = jnp.where((t - z >= 0) & (t - z < count), m, micro)
-            rows.append(jnp.stack([m, (z == 0).astype(m.dtype), place]))
+            rows.append(jnp.stack([m, (z == 0).astype(m.dtype)]))
         return jnp.stack(rows).astype(jnp.int32)
+
+    def place(stream, t):
+        m = t - z
+        return jnp.where((m >= 0) & (m < counts[stream]), stream + STREAMS * m, micro)
 
     counts = [len(range(a, micro, STREAMS)) for a in range(STREAMS)]
     idx = [indices(a, counts[a]) for a in range(STREAMS)]
     line = Line()
     result = [jnp.zeros((micro + 1, tok, width), BF)]
     state = [{} for _ in range(STREAMS)]
-
-    x_busy = []
-
-    def on_x():
-        return x_busy[-1] if x_busy else []
 
     def enter(a, t, s):
         given = [idx[a], gain_row, table]
@@ -241,21 +246,19 @@
 
     def tighten(a, t, s):
         (own,) = line.call(tighten_kernel, [column], s["rows"], "tighten")
-        if GATHER:
-            s["all"] = [lax.all_gather(own, ("x", "core"), tiled=True)]
-        else:
-            mine = [own] + [moved(own, "x", d) for d in range(1, 4)]
-            x_busy.append(mine[1:])
-            s["all"] = mine + [moved(v, "core", 1) for v in mine]
+        s["along_x"] = [own] + [moved(own, "x", d) for d in range(1, 4)]
+
+    def stack(a, t, s):
+        (s["mine"],) = line.call(stack_kernel, [(4 * slots, width)], s["along_x"], "stack")
+        s["theirs"] = moved(s["mine"], "core", 1)
 
     def experts(a, t, s):
-        s["keep"], give = line.experts(order, s["all"], w_up[0], w_down[0])
+        s["keep"], give = line.experts((s["mine"], s["theirs"]), w_up[0], w_down[0])
         s["back"] = moved(give, "core", 1)
 
     def pair(a, t, s):
         sums = line.call(pair_kernel, [column] * 4, [s["keep"], s["back"]], "pair")
         s["home"] = [sums[0]] + [moved(sums[d], "x", -d) for d in range(1, 4)]
-        x_busy.append(s["home"][1:])
 
     def spread(a, t, s):
         blocks = line.call(spread_kernel, [block] * 4, s["home"], "spread")
@@ -267,16 +270,16 @@
         )
         if t < counts[a] + SECTIONS - 2:
             s["from_before"] = lax.ppermute(made, "pipe", [(i, i + 1) for i in range(SECTIONS - 1)])
-        result[0] = lax.dynamic_update_index_in_dim(result[0], made, idx[a][t, 2], 0)
-
-    stages = (enter, tighten, experts, pair, spread, combine)
-    plan = []
-    for a in range(STREAMS):
-        for t in range(counts[a] + SECTIONS - 1):
-            for at, stage in zip(PHASES, stages):
-                plan.append((t * PERIOD + a * OFFSET + at, a, t, stage))
-    for _, a, t, stage in sorted(plan, key=lambda p: p[0]):
-        stage(a, t, state[a])
+        result[0] = lax.dynamic_update_index_in_dim(result[0], made, place(a, t), 0)
+
+    stages = (enter, tighten, stack, experts, pair, spread, combine)
+    done = [0] * STREAMS
+    n = (counts[0] + SECTIONS - 1) * len(stages)
+    lead = 1
+    for a in [0] * lead + [0, 1] * (n - lead) + [1] * lead:
+        t, i = divmod(done[a], len(stages))
+        done[a] += 1
+        stages[i](a, t, state[a])
     return result[0][None, :micro]
 
 

time: 779 us -> 749 us (0.961)
  waiting for transfers between devices: 246 us -> 338 us
  starting transfers between devices: 318 us -> 257 us
  local copies, waits for them, and re-layouts: 56.3 us -> 28.1 us
  between operations: 28.2 us -> 2.3 us
  Pallas kernels: 120 us -> 109 us
    ppermute x238 -> x196, waiting for transfers between devices: 240 us -> 315 us  [moved(): return lax.ppermute(value, axis, [(i, (i + by) % n) for i in range(n)])]
    ppermute x238 -> x196, starting transfers between devices: 276 us -> 234 us  [moved(): return lax.ppermute(value, axis, [(i, (i + by) % n) for i in range(n)])]
    ppermute x12, starting transfers between devices: 33.8 us -> 15.7 us  [combine(): lax.ppermute(made, 'pipe', [(i, i + 1) for i in range(SECTIONS - 1)])]
    unnamed x99 -> x81, local copies, waits for them, and re-layouts: 43.1 us -> 25.1 us
    ppermute x12, waiting for transfers between devices: 0.03 us -> 15.5 us  [combine(): lax.ppermute(made, 'pipe', [(i, i + 1) for i in range(SECTIONS - 1)])]
    pallas_call x82 -> x96, Pallas kernels: 120 us -> 109 us  [call(): pl.pallas_call(body, out_shape=[jax.ShapeDtypeStruct(s, BF) for s in outs...]
    slice x14 -> x0, local copies, waits for them, and re-layouts: 8.57 us -> none  [combine(): idx[a][t, 2]]
  transfers between devices with their start and end apart: 256 -> 214, of which waited for: 75 -> 111; matrix products, arithmetic and copies ran while one was open for 2% -> 1% of each run, Pallas kernels for 15% -> 11%
where the time goes in v2:
time: 749 us; the launch traced here: 740 us
  waiting for transfers between devices  338 us (45%)
  starting transfers between devices  257 us (34%)
  Pallas kernels  109 us (15%)
  local copies, waits for them, and re-layouts  28.1 us (4%)
    ppermute x196, waiting for transfers between devices, moved(): return lax.ppermute(value, axis, [(i, (i + by) % n) for i in range(n)])  315 us
    ppermute x196, starting transfers between devices, moved(): return lax.ppermute(value, axis, [(i, (i + by) % n) for i in range(n)])  234 us
    pallas_call x96, Pallas kernels, call(): pl.pallas_call(body, out_shape=[jax.ShapeDtypeStruct(s, BF) for s in outs...  109 us
    unnamed x81, local copies, waits for them, and re-layouts  25.1 us
    ppermute x12, starting transfers between devices, combine(): lax.ppermute(made, 'pipe', [(i, i + 1) for i in range(SECTIONS - 1)])  15.7 us
    ppermute x12, waiting for transfers between devices, combine(): lax.ppermute(made, 'pipe', [(i, i + 1) for i in range(SECTIONS - 1)])  15.5 us
  transfers between devices with their start and end apart: 214, of which 111 were waited for; matrix products, arithmetic and copies ran while one was open for 1% of the time, Pallas kernels for 11%

profile of v2, /device:TPU:1, one launch (start us, length us, event | category | flops | bytes accessed | tf_op | source)
XLA Modules:
  0.0 739.9 jit_solution(7449903282945425044)
XLA Ops:
  31.9 7.3 collective-permute-done.7.refs_2_
  63.6 5.2 experts.14
  75.1 5.2 experts.15
  82.7 6.5 collective-permute-done.17.refs_1_
  90.5 6.9 collective-permute-done.19.refs_3_
  166.1 5.2 experts.16
  182.0 5.2 experts.17
  190.9 5.5 collective-permute-done.50.refs_1_
  199.4 7.1 collective-permute-done.52.refs_3_
  220.9 5.3 collective-permute-done.60.refs_3_
  275.2 5.8 collective-permute-done.78.refs_2_
  285.6 5.2 experts.19
  294.0 6.1 collective-permute-done.80.refs_1_
  303.1 6.5 collective-permute-done.82.refs_3_
  322.9 7.0 collective-permute-done.90.refs_3_
  371.8 5.2 experts.20
  388.6 5.2 experts.21
  397.2 11.9 %collective-permute-done.110.refs_1_ = bf16[24,6144]{1,0:T(8,128)(2,1)S(1)} collective-permute-done((bf16[24,6144]{1,0:T(8,128)(2,1)S(1)}, bf16[24,6144]{1,0:T(8,128)(2,1)S(1)}, u32[]{:S(2)}, u32[]{:S(2)}) %collective-permute-start.110) | collective-permute-done | bytes 294944 | tf_op jit(solution)/shard_map/ppermute | solution.py:30
  427.6 6.2 collective-permute-done.120.refs_3_
  475.6 5.2 experts.22
  482.5 5.5 collective-permute-done.138.refs_2_
  492.8 5.2 experts.23
  501.3 11.9 %collective-permute-done.140.refs_1_ = bf16[24,6144]{1,0:T(8,128)(2,1)S(1)} collective-permute-done((bf16[24,6144]{1,0:T(8,128)(2,1)S(1)}, bf16[24,6144]{1,0:T(8,128)(2,1)S(1)}, u32[]{:S(2)}, u32[]{:S(2)}) %collective-permute-start.140) | collective-permute-done | bytes 294944 | tf_op jit(solution)/shard_map/ppermute | solution.py:30
  530.4 7.0 collective-permute-done.150.refs_3_
  558.3 6.9 collective-permute-done.158.refs_1_
  589.3 5.2 experts.24
  607.4 5.2 experts.25
  629.5 7.4 collective-permute-done.180.refs_3_
  672.2 5.2 experts.26
  690.2 5.2 experts.27
  699.1 6.8 collective-permute-done.202.refs_3_
  717.4 8.6 %collective-permute-done.210.refs_3_ = bf16[24,6144]{1,0:T(8,128)(2,1)S(1)} collective-permute-done((bf16[24,6144]{1,0:T(8,128)(2,1)S(1)}, bf16[24,6144]{1,0:T(8,128)(2,1)S(1)}, u32[]{:S(2)}, u32[]{:S(2)}) %collective-permute-start.210) | collective-permute-done | bytes 294944 | tf_op jit(solution)/shard_map/ppermute | solution.py:30
  (616 shorter events, 534.1 us)
Async XLA Ops:
  49.9 21.0 %collective-permute-start.14 = (bf16[24,6144]{1,0:T(8,128)(2,1)S(1)}, bf16[24,6144]{1,0:T(8,128)(2,1)S(1)}, u32[]{:S(2)}, u32[]{:S(2)}) collective-permute-start(bf16[24,6144]{1,0:T(8,128)(2,1)S(1)} %get-tuple-element.372.refs_0_), channel_id=1, source_target_pairs={{0,2},{2,4},{4,6},{6,0},{1,3},{3,5},{5,7},{7,1},{8,10},{10,12},{12... | collective-permute-start | bytes 884744 | tf_op jit(solution)/shard_map/ppermute | solution.py:30
  51.0 19.9 %collective-permute-start.15 = (bf16[24,6144]{1,0:T(8,128)(2,1)S(1)}, bf16[24,6144]{1,0:T(8,128)(2,1)S(1)}, u32[]{:S(2)}, u32[]{:S(2)}) collective-permute-start(bf16[24,6144]{1,0:T(8,128)(2,1)S(1)} %get-tuple-element.372.refs_0_), channel_id=1, source_target_pairs={{0,4},{2,6},{4,0},{6,2},{1,5},{3,7},{5,1},{7,3},{8,12},{10,14},{12... | collective-permute-start | bytes 884744 | tf_op jit(solution)/shard_map/ppermute | solution.py:30
  53.1 17.8 %collective-permute-start.16 = (bf16[24,6144]{1,0:T(8,128)(2,1)S(1)}, bf16[24,6144]{1,0:T(8,128)(2,1)S(1)}, u32[]{:S(2)}, u32[]{:S(2)}) collective-permute-start(bf16[24,6144]{1,0:T(8,128)(2,1)S(1)} %get-tuple-element.372.refs_0_), channel_id=1, source_target_pairs={{0,6},{2,0},{4,2},{6,4},{1,7},{3,1},{5,3},{7,5},{8,14},{10,8},{12,... | collective-permute-start | bytes 884744 | tf_op jit(solution)/shard_map/ppermute | solution.py:30
  80.2 17.5 %collective-permute-start.24 = (bf16[96,6144]{1,0:T(8,128)(2,1)S(1)}, bf16[96,6144]{1,0:T(8,128)(2,1)S(1)}, u32[]{:S(2)}, u32[]{:S(2)}) collective-permute-start(bf16[96,6144]{1,0:T(8,128)(2,1)S(1)} %get-tuple-element.387), channel_id=1, source_target_pairs={{0,1},{1,0},{2,3},{3,2},{4,5},{5,4},{6,7},{7,6},{8,9},{9,8},{10,11... | collective-permute-start | bytes 3538952 | tf_op jit(solution)/shard_map/ppermute | solution.py:30
  103.3 15.8 %collective-permute-start.32 = (bf16[6,16,1536]{2,1,0:T(8,128)(2,1)S(1)}, bf16[6,16,1536]{2,1,0:T(8,128)(2,1)S(1)}, u32[]{:S(2)}, u32[]{:S(2)}) collective-permute-start(bf16[6,16,1536]{2,1,0:T(8,128)(2,1)S(1)} %slice.10.refs_4_), channel_id=1, source_target_pairs={{32,0},{33,1},{34,2},{35,3},{36,4},{37,5},{38,6},{39,7},{40,8},{41... | collective-permute-start | bytes 884744 | tf_op jit(solution)/shard_map/ppermute | solution.py:201
  107.4 17.2 %collective-permute-start.34 = (bf16[6,16,1536]{2,1,0:T(8,128)(2,1)S(1)}, bf16[6,16,1536]{2,1,0:T(8,128)(2,1)S(1)}, u32[]{:S(2)}, u32[]{:S(2)}) collective-permute-start(bf16[6,16,1536]{2,1,0:T(8,128)(2,1)S(1)} %slice.10.refs_4_), channel_id=1, source_target_pairs={{96,0},{97,1},{98,2},{99,3},{100,4},{101,5},{102,6},{103,7},{104,8... | collective-permute-start | bytes 884744 | tf_op jit(solution)/shard_map/ppermute | solution.py:201
  150.4 15.7 %collective-permute-start.42 = (bf16[96,6144]{1,0:T(8,128)(2,1)S(1)}, bf16[96,6144]{1,0:T(8,128)(2,1)S(1)}, u32[]{:S(2)}, u32[]{:S(2)}) collective-permute-start(bf16[96,6144]{1,0:T(8,128)(2,1)S(1)} %get-tuple-element.413.refs_0_), channel_id=1, source_target_pairs={{0,1},{1,0},{2,3},{3,2},{4,5},{5,4},{6,7},{7,6},{8,9},{9,8},{10,11... | collective-permute-start | bytes 3538952 | tf_op jit(solution)/shard_map/ppermute | solution.py:30
  187.2 21.9 %collective-permute-start.57 = (bf16[96,6144]{1,0:T(8,128)(2,1)S(1)}, bf16[96,6144]{1,0:T(8,128)(2,1)S(1)}, u32[]{:S(2)}, u32[]{:S(2)}) collective-permute-start(bf16[96,6144]{1,0:T(8,128)(2,1)S(1)} %get-tuple-element.437), channel_id=1, source_target_pairs={{0,1},{1,0},{2,3},{3,2},{4,5},{5,4},{6,7},{7,6},{8,9},{9,8},{10,11... | collective-permute-start | bytes 3538952 | tf_op jit(solution)/shard_map/ppermute | solution.py:30
  190.6 15.9 %collective-permute-start.52 = (bf16[24,6144]{1,0:T(8,128)(2,1)S(1)}, bf16[24,6144]{1,0:T(8,128)(2,1)S(1)}, u32[]{:S(2)}, u32[]{:S(2)}) collective-permute-start(bf16[24,6144]{1,0:T(8,128)(2,1)S(1)} %get-tuple-element.428), channel_id=1, source_target_pairs={{0,2},{2,4},{4,6},{6,0},{1,3},{3,5},{5,7},{7,1},{8,10},{10,12},{12... | collective-permute-start | bytes 884744 | tf_op jit(solution)/shard_map/ppermute | solution.py:30
  210.3 15.9 %collective-permute-start.60 = (bf16[24,6144]{1,0:T(8,128)(2,1)S(1)}, bf16[24,6144]{1,0:T(8,128)(2,1)S(1)}, u32[]{:S(2)}, u32[]{:S(2)}) collective-permute-start(bf16[24,6144]{1,0:T(8,128)(2,1)S(1)} %get-tuple-element.445), channel_id=1, source_target_pairs={{0,2},{2,4},{4,6},{6,0},{1,3},{3,5},{5,7},{7,1},{8,10},{10,12},{12... | collective-permute-start | bytes 884744 | tf_op jit(solution)/shard_map/ppermute | solution.py:30
  265.3 15.8 %collective-permute-start.78 = (bf16[24,6144]{1,0:T(8,128)(2,1)S(1)}, bf16[24,6144]{1,0:T(8,128)(2,1)S(1)}, u32[]{:S(2)}, u32[]{:S(2)}) collective-permute-start(bf16[24,6144]{1,0:T(8,128)(2,1)S(1)} %get-tuple-element.472.refs_0_), channel_id=1, source_target_pairs={{0,4},{2,6},{4,0},{6,2},{1,5},{3,7},{5,1},{7,3},{8,12},{10,14},{12... | collective-permute-start | bytes 884744 | tf_op jit(solution)/shard_map/ppermute | solution.py:30
  290.8 21.9 %collective-permute-start.87 = (bf16[96,6144]{1,0:T(8,128)(2,1)S(1)}, bf16[96,6144]{1,0:T(8,128)(2,1)S(1)}, u32[]{:S(2)}, u32[]{:S(2)}) collective-permute-start(bf16[96,6144]{1,0:T(8,128)(2,1)S(1)} %get-tuple-element.487), channel_id=1, source_target_pairs={{0,1},{1,0},{2,3},{3,2},{4,5},{5,4},{6,7},{7,6},{8,9},{9,8},{10,11... | collective-permute-start | bytes 3538952 | tf_op jit(solution)/shard_map/ppermute | solution.py:30
  293.4 16.2 %collective-permute-start.82 = (bf16[24,6144]{1,0:T(8,128)(2,1)S(1)}, bf16[24,6144]{1,0:T(8,128)(2,1)S(1)}, u32[]{:S(2)}, u32[]{:S(2)}) collective-permute-start(bf16[24,6144]{1,0:T(8,128)(2,1)S(1)} %get-tuple-element.478), channel_id=1, source_target_pairs={{0,2},{2,4},{4,6},{6,0},{1,3},{3,5},{5,7},{7,1},{8,10},{10,12},{12... | collective-permute-start | bytes 884744 | tf_op jit(solution)/shard_map/ppermute | solution.py:30
  313.7 16.2 %collective-permute-start.90 = (bf16[24,6144]{1,0:T(8,128)(2,1)S(1)}, bf16[24,6144]{1,0:T(8,128)(2,1)S(1)}, u32[]{:S(2)}, u32[]{:S(2)}) collective-permute-start(bf16[24,6144]{1,0:T(8,128)(2,1)S(1)} %get-tuple-element.495), channel_id=1, source_target_pairs={{0,2},{2,4},{4,6},{6,0},{1,3},{3,5},{5,7},{7,1},{8,10},{10,12},{12... | collective-permute-start | bytes 884744 | tf_op jit(solution)/shard_map/ppermute | solution.py:30
  355.8 16.0 %collective-permute-start.102 = (bf16[96,6144]{1,0:T(8,128)(2,1)S(1)}, bf16[96,6144]{1,0:T(8,128)(2,1)S(1)}, u32[]{:S(2)}, u32[]{:S(2)}) collective-permute-start(bf16[96,6144]{1,0:T(8,128)(2,1)S(1)} %get-tuple-element.513.refs_0_), channel_id=1, source_target_pairs={{0,1},{1,0},{2,3},{3,2},{4,5},{5,4},{6,7},{7,6},{8,9},{9,8},{10,11... | collective-permute-start | bytes 3538952 | tf_op jit(solution)/shard_map/ppermute | solution.py:30
  393.8 22.8 %collective-permute-start.117 = (bf16[96,6144]{1,0:T(8,128)(2,1)S(1)}, bf16[96,6144]{1,0:T(8,128)(2,1)S(1)}, u32[]{:S(2)}, u32[]{:S(2)}) collective-permute-start(bf16[96,6144]{1,0:T(8,128)(2,1)S(1)} %get-tuple-element.537), channel_id=1, source_target_pairs={{0,1},{1,0},{2,3},{3,2},{4,5},{5,4},{6,7},{7,6},{8,9},{9,8},{10,11... | collective-permute-start | bytes 3538952 | tf_op jit(solution)/shard_map/ppermute | solution.py:30
  394.3 14.8 %collective-permute-start.110 = (bf16[24,6144]{1,0:T(8,128)(2,1)S(1)}, bf16[24,6144]{1,0:T(8,128)(2,1)S(1)}, u32[]{:S(2)}, u32[]{:S(2)}) collective-permute-start(bf16[24,6144]{1,0:T(8,128)(2,1)S(1)} %get-tuple-element.526), channel_id=1, source_target_pairs={{0,6},{2,0},{4,2},{6,4},{1,7},{3,1},{5,3},{7,5},{8,14},{10,8},{12,... | collective-permute-start | bytes 884744 | tf_op jit(solution)/shard_map/ppermute | solution.py:30
  397.1 16.3 %collective-permute-start.112 = (bf16[24,6144]{1,0:T(8,128)(2,1)S(1)}, bf16[24,6144]{1,0:T(8,128)(2,1)S(1)}, u32[]{:S(2)}, u32[]{:S(2)}) collective-permute-start(bf16[24,6144]{1,0:T(8,128)(2,1)S(1)} %get-tuple-element.528), channel_id=1, source_target_pairs={{0,2},{2,4},{4,6},{6,0},{1,3},{3,5},{5,7},{7,1},{8,10},{10,12},{12... | collective-permute-start | bytes 884744 | tf_op jit(solution)/shard_map/ppermute | solution.py:30
  417.5 16.3 %collective-permute-start.120 = (bf16[24,6144]{1,0:T(8,128)(2,1)S(1)}, bf16[24,6144]{1,0:T(8,128)(2,1)S(1)}, u32[]{:S(2)}, u32[]{:S(2)}) collective-permute-start(bf16[24,6144]{1,0:T(8,128)(2,1)S(1)} %get-tuple-element.545), channel_id=1, source_target_pairs={{0,2},{2,4},{4,6},{6,0},{1,3},{3,5},{5,7},{7,1},{8,10},{10,12},{12... | collective-permute-start | bytes 884744 | tf_op jit(solution)/shard_map/ppermute | solution.py:30
  472.3 15.7 %collective-permute-start.138 = (bf16[24,6144]{1,0:T(8,128)(2,1)S(1)}, bf16[24,6144]{1,0:T(8,128)(2,1)S(1)}, u32[]{:S(2)}, u32[]{:S(2)}) collective-permute-start(bf16[24,6144]{1,0:T(8,128)(2,1)S(1)} %get-tuple-element.572.refs_0_), channel_id=1, source_target_pairs={{0,4},{2,6},{4,0},{6,2},{1,5},{3,7},{5,1},{7,3},{8,12},{10,14},{12... | collective-permute-start | bytes 884744 | tf_op jit(solution)/shard_map/ppermute | solution.py:30
  498.0 22.2 %collective-permute-start.147 = (bf16[96,6144]{1,0:T(8,128)(2,1)S(1)}, bf16[96,6144]{1,0:T(8,128)(2,1)S(1)}, u32[]{:S(2)}, u32[]{:S(2)}) collective-permute-start(bf16[96,6144]{1,0:T(8,128)(2,1)S(1)} %get-tuple-element.587), channel_id=1, source_target_pairs={{0,1},{1,0},{2,3},{3,2},{4,5},{5,4},{6,7},{7,6},{8,9},{9,8},{10,11... | collective-permute-start | bytes 3538952 | tf_op jit(solution)/shard_map/ppermute | solution.py:30
  500.7 16.2 %collective-permute-start.142 = (bf16[24,6144]{1,0:T(8,128)(2,1)S(1)}, bf16[24,6144]{1,0:T(8,128)(2,1)S(1)}, u32[]{:S(2)}, u32[]{:S(2)}) collective-permute-start(bf16[24,6144]{1,0:T(8,128)(2,1)S(1)} %get-tuple-element.578), channel_id=1, source_target_pairs={{0,2},{2,4},{4,6},{6,0},{1,3},{3,5},{5,7},{7,1},{8,10},{10,12},{12... | collective-permute-start | bytes 884744 | tf_op jit(solution)/shard_map/ppermute | solution.py:30
  521.2 16.2 %collective-permute-start.150 = (bf16[24,6144]{1,0:T(8,128)(2,1)S(1)}, bf16[24,6144]{1,0:T(8,128)(2,1)S(1)}, u32[]{:S(2)}, u32[]{:S(2)}) collective-permute-start(bf16[24,6144]{1,0:T(8,128)(2,1)S(1)} %get-tuple-element.595), channel_id=1, source_target_pairs={{0,2},{2,4},{4,6},{6,0},{1,3},{3,5},{5,7},{7,1},{8,10},{10,12},{12... | collective-permute-start | bytes 884744 | tf_op jit(solution)/shard_map/ppermute | solution.py:30
  550.2 15.0 %collective-permute-start.158 = (bf16[24,6144]{1,0:T(8,128)(2,1)S(1)}, bf16[24,6144]{1,0:T(8,128)(2,1)S(1)}, u32[]{:S(2)}, u32[]{:S(2)}) collective-permute-start(bf16[24,6144]{1,0:T(8,128)(2,1)S(1)} %get-tuple-element.610.refs_0_), channel_id=1, source_target_pairs={{0,2},{2,4},{4,6},{6,0},{1,3},{3,5},{5,7},{7,1},{8,10},{10,12},{12... | collective-permute-start | bytes 884744 | tf_op jit(solution)/shard_map/ppermute | solution.py:30
  550.3 15.0 %collective-permute-start.159 = (bf16[24,6144]{1,0:T(8,128)(2,1)S(1)}, bf16[24,6144]{1,0:T(8,128)(2,1)S(1)}, u32[]{:S(2)}, u32[]{:S(2)}) collective-permute-start(bf16[24,6144]{1,0:T(8,128)(2,1)S(1)} %get-tuple-element.610.refs_0_), channel_id=1, source_target_pairs={{0,4},{2,6},{4,0},{6,2},{1,5},{3,7},{5,1},{7,3},{8,12},{10,14},{12... | collective-permute-start | bytes 884744 | tf_op jit(solution)/shard_map/ppermute | solution.py:30
  551.3 14.9 %collective-permute-start.160 = (bf16[24,6144]{1,0:T(8,128)(2,1)S(1)}, bf16[24,6144]{1,0:T(8,128)(2,1)S(1)}, u32[]{:S(2)}, u32[]{:S(2)}) collective-permute-start(bf16[24,6144]{1,0:T(8,128)(2,1)S(1)} %get-tuple-element.610.refs_0_), channel_id=1, source_target_pairs={{0,6},{2,0},{4,2},{6,4},{1,7},{3,1},{5,3},{7,5},{8,14},{10,8},{12,... | collective-permute-start | bytes 884744 | tf_op jit(solution)/shard_map/ppermute | solution.py:30
  576.8 19.7 %collective-permute-start.167 = (bf16[24,6144]{1,0:T(8,128)(2,1)S(1)}, bf16[24,6144]{1,0:T(8,128)(2,1)S(1)}, u32[]{:S(2)}, u32[]{:S(2)}) collective-permute-start(bf16[24,6144]{1,0:T(8,128)(2,1)S(1)} %get-tuple-element.622.refs_0_), channel_id=1, source_target_pairs={{0,2},{2,4},{4,6},{6,0},{1,3},{3,5},{5,7},{7,1},{8,10},{10,12},{12... | collective-permute-start | bytes 884744 | tf_op jit(solution)/shard_map/ppermute | solution.py:30
  576.8 19.6 %collective-permute-start.168 = (bf16[24,6144]{1,0:T(8,128)(2,1)S(1)}, bf16[24,6144]{1,0:T(8,128)(2,1)S(1)}, u32[]{:S(2)}, u32[]{:S(2)}) collective-permute-start(bf16[24,6144]{1,0:T(8,128)(2,1)S(1)} %get-tuple-element.622.refs_0_), channel_id=1, source_target_pairs={{0,4},{2,6},{4,0},{6,2},{1,5},{3,7},{5,1},{7,3},{8,12},{10,14},{12... | collective-permute-start | bytes 884744 | tf_op jit(solution)/shard_map/ppermute | solution.py:30
  580.2 16.3 %collective-permute-start.169 = (bf16[24,6144]{1,0:T(8,128)(2,1)S(1)}, bf16[24,6144]{1,0:T(8,128)(2,1)S(1)}, u32[]{:S(2)}, u32[]{:S(2)}) collective-permute-start(bf16[24,6144]{1,0:T(8,128)(2,1)S(1)} %get-tuple-element.622.refs_0_), channel_id=1, source_target_pairs={{0,6},{2,0},{4,2},{6,4},{1,7},{3,1},{5,3},{7,5},{8,14},{10,8},{12,... | collective-permute-start | bytes 884744 | tf_op jit(solution)/shard_map/ppermute | solution.py:30
  669.4 15.4 %collective-permute-start.198 = (bf16[24,6144]{1,0:T(8,128)(2,1)S(1)}, bf16[24,6144]{1,0:T(8,128)(2,1)S(1)}, u32[]{:S(2)}, u32[]{:S(2)}) collective-permute-start(bf16[24,6144]{1,0:T(8,128)(2,1)S(1)} %get-tuple-element.672.refs_0_), channel_id=1, source_target_pairs={{0,4},{2,6},{4,0},{6,2},{1,5},{3,7},{5,1},{7,3},{8,12},{10,14},{12... | collective-permute-start | bytes 884744 | tf_op jit(solution)/shard_map/ppermute | solution.py:30
  689.2 16.6 %collective-permute-start.202 = (bf16[24,6144]{1,0:T(8,128)(2,1)S(1)}, bf16[24,6144]{1,0:T(8,128)(2,1)S(1)}, u32[]{:S(2)}, u32[]{:S(2)}) collective-permute-start(bf16[24,6144]{1,0:T(8,128)(2,1)S(1)} %get-tuple-element.678), channel_id=1, source_target_pairs={{0,2},{2,4},{4,6},{6,0},{1,3},{3,5},{5,7},{7,1},{8,10},{10,12},{12... | collective-permute-start | bytes 884744 | tf_op jit(solution)/shard_map/ppermute | solution.py:30
  710.0 16.0 %collective-permute-start.210 = (bf16[24,6144]{1,0:T(8,128)(2,1)S(1)}, bf16[24,6144]{1,0:T(8,128)(2,1)S(1)}, u32[]{:S(2)}, u32[]{:S(2)}) collective-permute-start(bf16[24,6144]{1,0:T(8,128)(2,1)S(1)} %get-tuple-element.695), channel_id=1, source_target_pairs={{0,2},{2,4},{4,6},{6,0},{1,3},{3,5},{5,7},{7,1},{8,10},{10,12},{12... | collective-permute-start | bytes 884744 | tf_op jit(solution)/shard_map/ppermute | solution.py:30
  (222 other events, 2164.3 us)

commit v3 on v2

--- a/solution.py
+++ b/solution.py
@@ -12,6 +12,8 @@
 PAD = 8
 STREAMS = 2
 COST = 1
+LEAD = 1
+PATTERN = (0, 1, 0, 0, 1, 0, 0, 1, 1, 0, 1, 1, 0, 1, 0, 1)
 SECTIONS = 4
 BF = jnp.bfloat16
 F32 = jnp.float32
@@ -85,6 +87,10 @@
     for d, out in enumerate(outs):
         total = own[...].astype(F32)[d * n : (d + 1) * n] + other[...].astype(F32)[d * n : (d + 1) * n]
         out[...] = total.astype(BF)
+
+
+def copy_kernel(given, made):
+    made[...] = given[...]
 
 
 def stack_kernel(own, r1, r2, r3, out):
@@ -140,6 +146,9 @@
         )(*args, self.token)
         return result
 
+    def mark(self, value):
+        return self.call(copy_kernel, [value.shape], [value], "mark")[0]
+
     def experts(self, rows, up, down):
         width, units = up.shape
         half = rows[0].shape[0]
@@ -163,30 +172,13 @@
     return jnp.where(chosen < EXPERTS, distance * PAD + rank, -1)
 
 
-STAGES = (
-    (1.0, 3.5, "y", 4.0, 3.5),
-    (0.3, 4.0, "x", 11.8, 2.5),
-    (0.5, 0.3, "core", 2.0, 0.8),
-    (5.9, 0.3, "core", 2.0, 0.8),
-    (0.4, 4.0, "x", 11.8, 2.5),
-    (0.3, 3.5, "y", 4.0, 3.5),
-    (0.9, 1.5, "pipe", 4.0, 4.0),
-)
-
-
 def planned(totals):
-    done, ready, links = [0] * len(totals), [0.0] * len(totals), {}
-    now, order = 0.0, []
-    while len(order) < sum(totals):
-        left = [a for a in range(len(totals)) if done[a] < totals[a]]
-        a = min(left, key=lambda a: (max(now, ready[a]), done[a] - totals[a]))
-        kernel, starts, link, busy, latency = STAGES[done[a] % len(STAGES)]
-        now = max(now, ready[a]) + kernel
-        links[link] = max(now + 0.4 * starts, links.get(link, 0.0)) + busy
-        ready[a] = max(links[link] + latency, now + starts)
-        now += starts
-        done[a] += 1
-        order.append(a)
+    order, left = [0] * LEAD, [totals[0] - LEAD, totals[1]]
+    while any(left):
+        for a in PATTERN:
+            if left[a]:
+                order.append(a)
+                left[a] -= 1
     return order
 
 
@@ -253,8 +245,10 @@
         s["theirs"] = moved(s["mine"], "core", 1)
 
     def experts(a, t, s):
-        s["keep"], give = line.experts((s["mine"], s["theirs"]), w_up[0], w_down[0])
-        s["back"] = moved(give, "core", 1)
+        s["keep"], s["give"] = line.experts((s["mine"], s["theirs"]), w_up[0], w_down[0])
+
+    def swap(a, t, s):
+        s["back"] = moved(line.mark(s["give"]), "core", 1)
 
     def pair(a, t, s):
         sums = line.call(pair_kernel, [column] * 4, [s["keep"], s["back"]], "pair")
@@ -272,11 +266,9 @@
             s["from_before"] = lax.ppermute(made, "pipe", [(i, i + 1) for i in range(SECTIONS - 1)])
         result[0] = lax.dynamic_update_index_in_dim(result[0], made, place(a, t), 0)
 
-    stages = (enter, tighten, stack, experts, pair, spread, combine)
+    stages = (enter, tighten, stack, experts, swap, pair, spread, combine)
     done = [0] * STREAMS
-    n = (counts[0] + SECTIONS - 1) * len(stages)
-    lead = 1
-    for a in [0] * lead + [0, 1] * (n - lead) + [1] * lead:
+    for a in planned([(c + SECTIONS - 1) * len(stages) for c in counts]):
         t, i = divmod(done[a], len(stages))
         done[a] += 1
         stages[i](a, t, state[a])

time: 749 us -> 749 us (level)
    pallas_call x96 -> x110, Pallas kernels: 109 us -> 111 us  [call(): pl.pallas_call(body, out_shape=[jax.ShapeDtypeStruct(s, BF) for s in outs...]
    unnamed x81 -> x77, local copies, waits for them, and re-layouts: 25.1 us -> 25.1 us
  transfers between devices with their start and end apart: 214 -> 214, of which waited for: 111 -> 115; matrix products, arithmetic and copies ran while one was open for 1% -> 1% of each run, Pallas kernels for 11% -> 14%
where the time goes in v3:
time: 749 us; the launch traced here: 740 us
  waiting for transfers between devices  342 us (46%)
  starting transfers between devices  252 us (34%)
  Pallas kernels  111 us (15%)
  local copies, waits for them, and re-layouts  28.1 us (4%)
    ppermute x196, waiting for transfers between devices, moved(): return lax.ppermute(value, axis, [(i, (i + by) % n) for i in range(n)])  321 us
    ppermute x196, starting transfers between devices, moved(): return lax.ppermute(value, axis, [(i, (i + by) % n) for i in range(n)])  228 us
    pallas_call x110, Pallas kernels, call(): pl.pallas_call(body, out_shape=[jax.ShapeDtypeStruct(s, BF) for s in outs...  111 us
    unnamed x77, local copies, waits for them, and re-layouts  25.1 us
    ppermute x12, starting transfers between devices, combine(): lax.ppermute(made, 'pipe', [(i, i + 1) for i in range(SECTIONS - 1)])  16.4 us
    ppermute x12, waiting for transfers between devices, combine(): lax.ppermute(made, 'pipe', [(i, i + 1) for i in range(SECTIONS - 1)])  15.5 us
  transfers between devices with their start and end apart: 214, of which 115 were waited for; matrix products, arithmetic and copies ran while one was open for 1% of the time, Pallas kernels for 14%

profile of v3, /device:TPU:1, one launch (start us, length us, event | category | flops | bytes accessed | tf_op | source)
XLA Modules:
  0.0 740.3 jit_solution(5174619554949390188)
XLA Ops:
  31.9 7.3 collective-permute-done.7.refs_2_
  71.3 6.8 collective-permute-done.18.refs_2_
  83.0 5.2 experts.15
  88.2 6.0 collective-permute-done.14.refs_1_
  145.3 6.2 collective-permute-done.39.refs_2_
  158.3 5.2 experts.16
  168.5 5.9 collective-permute-done.50.refs_1_
  174.5 7.2 collective-permute-done.51.refs_2_
  190.7 6.6 collective-permute-done.47.refs_1_
  216.6 5.8 collective-permute-done.60.refs_3_
  243.6 7.2 collective-permute-done.68.refs_1_
  267.6 6.2 collective-permute-done.80.refs_1_
  273.9 6.9 collective-permute-done.81.refs_2_
  284.9 5.2 experts.19
  290.1 6.6 collective-permute-done.77.refs_1_
  316.1 5.7 collective-permute-done.90.refs_3_
  366.7 6.1 collective-permute-done.110.refs_1_
  372.8 5.6 collective-permute-done.111.refs_2_
  388.9 6.4 collective-permute-done.107.refs_1_
  414.8 5.6 collective-permute-done.120.refs_3_
  465.7 6.3 collective-permute-done.140.refs_1_
  472.0 6.9 collective-permute-done.141.refs_2_
  488.2 6.6 collective-permute-done.137.refs_1_
  514.2 5.7 collective-permute-done.150.refs_3_
  564.8 5.2 experts.24
  579.2 6.9 collective-permute-done.171.refs_2_
  620.5 7.9 %collective-permute-done.180.refs_3_ = bf16[24,6144]{1,0:T(8,128)(2,1)S(1)} collective-permute-done((bf16[24,6144]{1,0:T(8,128)(2,1)S(1)}, bf16[24,6144]{1,0:T(8,128)(2,1)S(1)}, u32[]{:S(2)}, u32[]{:S(2)}) %collective-permute-start.180) | collective-permute-done | bytes 294944 | tf_op jit(solution)/shard_map/ppermute | solution.py:32
  664.9 5.2 experts.26
  677.0 9.2 %collective-permute-done.200.refs_1_ = bf16[24,6144]{1,0:T(8,128)(2,1)S(1)} collective-permute-done((bf16[24,6144]{1,0:T(8,128)(2,1)S(1)}, bf16[24,6144]{1,0:T(8,128)(2,1)S(1)}, u32[]{:S(2)}, u32[]{:S(2)}) %collective-permute-start.200) | collective-permute-done | bytes 294944 | tf_op jit(solution)/shard_map/ppermute | solution.py:32
  691.1 5.2 experts.27
  700.0 6.8 collective-permute-done.199.refs_3_
  720.5 7.3 collective-permute-done.210.refs_3_
  (626 shorter events, 534.9 us)
Async XLA Ops:
  41.7 18.4 %collective-permute-start.10 = (bf16[8,6144]{1,0:T(8,128)(2,1)S(1)}, bf16[8,6144]{1,0:T(8,128)(2,1)S(1)}, u32[]{:S(2)}, u32[]{:S(2)}) collective-permute-start(bf16[8,6144]{1,0:T(8,128)(2,1)S(1)} %get-tuple-element.396), channel_id=1, source_target_pairs={{0,8},{8,16},{16,24},{24,0},{1,9},{9,17},{17,25},{25,1},{2,10},{10... | collective-permute-start | bytes 294920 | tf_op jit(solution)/shard_map/ppermute | solution.py:32
  41.7 18.4 %collective-permute-start.11 = (bf16[8,6144]{1,0:T(8,128)(2,1)S(1)}, bf16[8,6144]{1,0:T(8,128)(2,1)S(1)}, u32[]{:S(2)}, u32[]{:S(2)}) collective-permute-start(bf16[8,6144]{1,0:T(8,128)(2,1)S(1)} %get-tuple-element.397), channel_id=1, source_target_pairs={{0,16},{8,24},{16,0},{24,8},{1,17},{9,25},{17,1},{25,9},{2,18},{10... | collective-permute-start | bytes 294920 | tf_op jit(solution)/shard_map/ppermute | solution.py:32
  44.5 15.7 %collective-permute-start.12 = (bf16[8,6144]{1,0:T(8,128)(2,1)S(1)}, bf16[8,6144]{1,0:T(8,128)(2,1)S(1)}, u32[]{:S(2)}, u32[]{:S(2)}) collective-permute-start(bf16[8,6144]{1,0:T(8,128)(2,1)S(1)} %get-tuple-element.398), channel_id=1, source_target_pairs={{0,24},{8,0},{16,8},{24,16},{1,25},{9,1},{17,9},{25,17},{2,26},{10... | collective-permute-start | bytes 294920 | tf_op jit(solution)/shard_map/ppermute | solution.py:32
  82.9 15.9 %collective-permute-start.16 = (bf16[24,6144]{1,0:T(8,128)(2,1)S(1)}, bf16[24,6144]{1,0:T(8,128)(2,1)S(1)}, u32[]{:S(2)}, u32[]{:S(2)}) collective-permute-start(bf16[24,6144]{1,0:T(8,128)(2,1)S(1)} %get-tuple-element.406), channel_id=1, source_target_pairs={{0,2},{2,4},{4,6},{6,0},{1,3},{3,5},{5,7},{7,1},{8,10},{10,12},{12... | collective-permute-start | bytes 884744 | tf_op jit(solution)/shard_map/ppermute | solution.py:32
  106.7 16.4 %collective-permute-start.32 = (bf16[6,16,1536]{2,1,0:T(8,128)(2,1)S(1)}, bf16[6,16,1536]{2,1,0:T(8,128)(2,1)S(1)}, u32[]{:S(2)}, u32[]{:S(2)}) collective-permute-start(bf16[6,16,1536]{2,1,0:T(8,128)(2,1)S(1)} %slice.10.refs_4_), channel_id=1, source_target_pairs={{32,0},{33,1},{34,2},{35,3},{36,4},{37,5},{38,6},{39,7},{40,8},{41... | collective-permute-start | bytes 884744 | tf_op jit(solution)/shard_map/ppermute | solution.py:193
  108.0 16.0 %collective-permute-start.33 = (bf16[6,16,1536]{2,1,0:T(8,128)(2,1)S(1)}, bf16[6,16,1536]{2,1,0:T(8,128)(2,1)S(1)}, u32[]{:S(2)}, u32[]{:S(2)}) collective-permute-start(bf16[6,16,1536]{2,1,0:T(8,128)(2,1)S(1)} %slice.10.refs_4_), channel_id=1, source_target_pairs={{64,0},{65,1},{66,2},{67,3},{68,4},{69,5},{70,6},{71,7},{72,8},{73... | collective-permute-start | bytes 884744 | tf_op jit(solution)/shard_map/ppermute | solution.py:193
  110.1 16.6 %collective-permute-start.34 = (bf16[6,16,1536]{2,1,0:T(8,128)(2,1)S(1)}, bf16[6,16,1536]{2,1,0:T(8,128)(2,1)S(1)}, u32[]{:S(2)}, u32[]{:S(2)}) collective-permute-start(bf16[6,16,1536]{2,1,0:T(8,128)(2,1)S(1)} %slice.10.refs_4_), channel_id=1, source_target_pairs={{96,0},{97,1},{98,2},{99,3},{100,4},{101,5},{102,6},{103,7},{104,8... | collective-permute-start | bytes 884744 | tf_op jit(solution)/shard_map/ppermute | solution.py:193
  165.5 16.1 %collective-permute-start.51 = (bf16[24,6144]{1,0:T(8,128)(2,1)S(1)}, bf16[24,6144]{1,0:T(8,128)(2,1)S(1)}, u32[]{:S(2)}, u32[]{:S(2)}) collective-permute-start(bf16[24,6144]{1,0:T(8,128)(2,1)S(1)} %get-tuple-element.461.refs_0_), channel_id=1, source_target_pairs={{0,4},{2,6},{4,0},{6,2},{1,5},{3,7},{5,1},{7,3},{8,12},{10,14},{12... | collective-permute-start | bytes 884744 | tf_op jit(solution)/shard_map/ppermute | solution.py:32
  185.1 16.5 %collective-permute-start.49 = (bf16[24,6144]{1,0:T(8,128)(2,1)S(1)}, bf16[24,6144]{1,0:T(8,128)(2,1)S(1)}, u32[]{:S(2)}, u32[]{:S(2)}) collective-permute-start(bf16[24,6144]{1,0:T(8,128)(2,1)S(1)} %get-tuple-element.460), channel_id=1, source_target_pairs={{0,2},{2,4},{4,6},{6,0},{1,3},{3,5},{5,7},{7,1},{8,10},{10,12},{12... | collective-permute-start | bytes 884744 | tf_op jit(solution)/shard_map/ppermute | solution.py:32
  205.9 16.5 %collective-permute-start.60 = (bf16[24,6144]{1,0:T(8,128)(2,1)S(1)}, bf16[24,6144]{1,0:T(8,128)(2,1)S(1)}, u32[]{:S(2)}, u32[]{:S(2)}) collective-permute-start(bf16[24,6144]{1,0:T(8,128)(2,1)S(1)} %get-tuple-element.481), channel_id=1, source_target_pairs={{0,2},{2,4},{4,6},{6,0},{1,3},{3,5},{5,7},{7,1},{8,10},{10,12},{12... | collective-permute-start | bytes 884744 | tf_op jit(solution)/shard_map/ppermute | solution.py:32
  264.1 16.7 %collective-permute-start.81 = (bf16[24,6144]{1,0:T(8,128)(2,1)S(1)}, bf16[24,6144]{1,0:T(8,128)(2,1)S(1)}, u32[]{:S(2)}, u32[]{:S(2)}) collective-permute-start(bf16[24,6144]{1,0:T(8,128)(2,1)S(1)} %get-tuple-element.515.refs_0_), channel_id=1, source_target_pairs={{0,4},{2,6},{4,0},{6,2},{1,5},{3,7},{5,1},{7,3},{8,12},{10,14},{12... | collective-permute-start | bytes 884744 | tf_op jit(solution)/shard_map/ppermute | solution.py:32
  284.2 16.5 %collective-permute-start.79 = (bf16[24,6144]{1,0:T(8,128)(2,1)S(1)}, bf16[24,6144]{1,0:T(8,128)(2,1)S(1)}, u32[]{:S(2)}, u32[]{:S(2)}) collective-permute-start(bf16[24,6144]{1,0:T(8,128)(2,1)S(1)} %get-tuple-element.514), channel_id=1, source_target_pairs={{0,2},{2,4},{4,6},{6,0},{1,3},{3,5},{5,7},{7,1},{8,10},{10,12},{12... | collective-permute-start | bytes 884744 | tf_op jit(solution)/shard_map/ppermute | solution.py:32
  305.1 16.8 %collective-permute-start.90 = (bf16[24,6144]{1,0:T(8,128)(2,1)S(1)}, bf16[24,6144]{1,0:T(8,128)(2,1)S(1)}, u32[]{:S(2)}, u32[]{:S(2)}) collective-permute-start(bf16[24,6144]{1,0:T(8,128)(2,1)S(1)} %get-tuple-element.535), channel_id=1, source_target_pairs={{0,2},{2,4},{4,6},{6,0},{1,3},{3,5},{5,7},{7,1},{8,10},{10,12},{12... | collective-permute-start | bytes 884744 | tf_op jit(solution)/shard_map/ppermute | solution.py:32
  362.6 15.7 %collective-permute-start.111 = (bf16[24,6144]{1,0:T(8,128)(2,1)S(1)}, bf16[24,6144]{1,0:T(8,128)(2,1)S(1)}, u32[]{:S(2)}, u32[]{:S(2)}) collective-permute-start(bf16[24,6144]{1,0:T(8,128)(2,1)S(1)} %get-tuple-element.569.refs_0_), channel_id=1, source_target_pairs={{0,4},{2,6},{4,0},{6,2},{1,5},{3,7},{5,1},{7,3},{8,12},{10,14},{12... | collective-permute-start | bytes 884744 | tf_op jit(solution)/shard_map/ppermute | solution.py:32
  383.2 16.3 %collective-permute-start.109 = (bf16[24,6144]{1,0:T(8,128)(2,1)S(1)}, bf16[24,6144]{1,0:T(8,128)(2,1)S(1)}, u32[]{:S(2)}, u32[]{:S(2)}) collective-permute-start(bf16[24,6144]{1,0:T(8,128)(2,1)S(1)} %get-tuple-element.568), channel_id=1, source_target_pairs={{0,2},{2,4},{4,6},{6,0},{1,3},{3,5},{5,7},{7,1},{8,10},{10,12},{12... | collective-permute-start | bytes 884744 | tf_op jit(solution)/shard_map/ppermute | solution.py:32
  404.1 16.3 %collective-permute-start.120 = (bf16[24,6144]{1,0:T(8,128)(2,1)S(1)}, bf16[24,6144]{1,0:T(8,128)(2,1)S(1)}, u32[]{:S(2)}, u32[]{:S(2)}) collective-permute-start(bf16[24,6144]{1,0:T(8,128)(2,1)S(1)} %get-tuple-element.589), channel_id=1, source_target_pairs={{0,2},{2,4},{4,6},{6,0},{1,3},{3,5},{5,7},{7,1},{8,10},{10,12},{12... | collective-permute-start | bytes 884744 | tf_op jit(solution)/shard_map/ppermute | solution.py:32
  462.2 16.7 %collective-permute-start.141 = (bf16[24,6144]{1,0:T(8,128)(2,1)S(1)}, bf16[24,6144]{1,0:T(8,128)(2,1)S(1)}, u32[]{:S(2)}, u32[]{:S(2)}) collective-permute-start(bf16[24,6144]{1,0:T(8,128)(2,1)S(1)} %get-tuple-element.623.refs_0_), channel_id=1, source_target_pairs={{0,4},{2,6},{4,0},{6,2},{1,5},{3,7},{5,1},{7,3},{8,12},{10,14},{12... | collective-permute-start | bytes 884744 | tf_op jit(solution)/shard_map/ppermute | solution.py:32
  482.3 16.5 %collective-permute-start.139 = (bf16[24,6144]{1,0:T(8,128)(2,1)S(1)}, bf16[24,6144]{1,0:T(8,128)(2,1)S(1)}, u32[]{:S(2)}, u32[]{:S(2)}) collective-permute-start(bf16[24,6144]{1,0:T(8,128)(2,1)S(1)} %get-tuple-element.622), channel_id=1, source_target_pairs={{0,2},{2,4},{4,6},{6,0},{1,3},{3,5},{5,7},{7,1},{8,10},{10,12},{12... | collective-permute-start | bytes 884744 | tf_op jit(solution)/shard_map/ppermute | solution.py:32
  503.2 16.8 %collective-permute-start.150 = (bf16[24,6144]{1,0:T(8,128)(2,1)S(1)}, bf16[24,6144]{1,0:T(8,128)(2,1)S(1)}, u32[]{:S(2)}, u32[]{:S(2)}) collective-permute-start(bf16[24,6144]{1,0:T(8,128)(2,1)S(1)} %get-tuple-element.643), channel_id=1, source_target_pairs={{0,2},{2,4},{4,6},{6,0},{1,3},{3,5},{5,7},{7,1},{8,10},{10,12},{12... | collective-permute-start | bytes 884744 | tf_op jit(solution)/shard_map/ppermute | solution.py:32
  552.4 17.7 %collective-permute-start.163 = (bf16[8,6144]{1,0:T(8,128)(2,1)}, bf16[8,6144]{1,0:T(8,128)(2,1)S(1)}, u32[]{:S(2)}, u32[]{:S(2)}) collective-permute-start(bf16[8,6144]{1,0:T(8,128)(2,1)} %get-tuple-element.666), channel_id=1, source_target_pairs={{0,8},{8,16},{16,24},{24,0},{1,9},{9,17},{17,25},{25,1},{2,10},{10... | collective-permute-start | bytes 294920 | tf_op jit(solution)/shard_map/ppermute | solution.py:32
  552.4 17.7 %collective-permute-start.164 = (bf16[8,6144]{1,0:T(8,128)(2,1)}, bf16[8,6144]{1,0:T(8,128)(2,1)S(1)}, u32[]{:S(2)}, u32[]{:S(2)}) collective-permute-start(bf16[8,6144]{1,0:T(8,128)(2,1)} %get-tuple-element.667), channel_id=1, source_target_pairs={{0,16},{8,24},{16,0},{24,8},{1,17},{9,25},{17,1},{25,9},{2,18},{10... | collective-permute-start | bytes 294920 | tf_op jit(solution)/shard_map/ppermute | solution.py:32
  570.4 15.7 %collective-permute-start.171 = (bf16[24,6144]{1,0:T(8,128)(2,1)S(1)}, bf16[24,6144]{1,0:T(8,128)(2,1)S(1)}, u32[]{:S(2)}, u32[]{:S(2)}) collective-permute-start(bf16[24,6144]{1,0:T(8,128)(2,1)S(1)} %get-tuple-element.677.refs_0_), channel_id=1, source_target_pairs={{0,4},{2,6},{4,0},{6,2},{1,5},{3,7},{5,1},{7,3},{8,12},{10,14},{12... | collective-permute-start | bytes 884744 | tf_op jit(solution)/shard_map/ppermute | solution.py:32
  590.5 16.5 %collective-permute-start.169 = (bf16[24,6144]{1,0:T(8,128)(2,1)S(1)}, bf16[24,6144]{1,0:T(8,128)(2,1)S(1)}, u32[]{:S(2)}, u32[]{:S(2)}) collective-permute-start(bf16[24,6144]{1,0:T(8,128)(2,1)S(1)} %get-tuple-element.676), channel_id=1, source_target_pairs={{0,2},{2,4},{4,6},{6,0},{1,3},{3,5},{5,7},{7,1},{8,10},{10,12},{12... | collective-permute-start | bytes 884744 | tf_op jit(solution)/shard_map/ppermute | solution.py:32
  612.5 16.0 %collective-permute-start.180 = (bf16[24,6144]{1,0:T(8,128)(2,1)S(1)}, bf16[24,6144]{1,0:T(8,128)(2,1)S(1)}, u32[]{:S(2)}, u32[]{:S(2)}) collective-permute-start(bf16[24,6144]{1,0:T(8,128)(2,1)S(1)} %get-tuple-element.697), channel_id=1, source_target_pairs={{0,2},{2,4},{4,6},{6,0},{1,3},{3,5},{5,7},{7,1},{8,10},{10,12},{12... | collective-permute-start | bytes 884744 | tf_op jit(solution)/shard_map/ppermute | solution.py:32
  642.8 17.2 %collective-permute-start.189 = (bf16[24,6144]{1,0:T(8,128)(2,1)S(1)}, bf16[24,6144]{1,0:T(8,128)(2,1)S(1)}, u32[]{:S(2)}, u32[]{:S(2)}) collective-permute-start(bf16[24,6144]{1,0:T(8,128)(2,1)S(1)} %get-tuple-element.712.refs_0_), channel_id=1, source_target_pairs={{0,4},{2,6},{4,0},{6,2},{1,5},{3,7},{5,1},{7,3},{8,12},{10,14},{12... | collective-permute-start | bytes 884744 | tf_op jit(solution)/shard_map/ppermute | solution.py:32
  642.9 17.1 %collective-permute-start.190 = (bf16[24,6144]{1,0:T(8,128)(2,1)S(1)}, bf16[24,6144]{1,0:T(8,128)(2,1)S(1)}, u32[]{:S(2)}, u32[]{:S(2)}) collective-permute-start(bf16[24,6144]{1,0:T(8,128)(2,1)S(1)} %get-tuple-element.712.refs_0_), channel_id=1, source_target_pairs={{0,6},{2,0},{4,2},{6,4},{1,7},{3,1},{5,3},{7,5},{8,14},{10,8},{12,... | collective-permute-start | bytes 884744 | tf_op jit(solution)/shard_map/ppermute | solution.py:32
  650.4 19.7 %collective-permute-start.193 = (bf16[8,6144]{1,0:T(8,128)(2,1)S(1)}, bf16[8,6144]{1,0:T(8,128)(2,1)S(1)}, u32[]{:S(2)}, u32[]{:S(2)}) collective-permute-start(bf16[8,6144]{1,0:T(8,128)(2,1)S(1)} %get-tuple-element.720), channel_id=1, source_target_pairs={{0,8},{8,16},{16,24},{24,0},{1,9},{9,17},{17,25},{25,1},{2,10},{10... | collective-permute-start | bytes 294920 | tf_op jit(solution)/shard_map/ppermute | solution.py:32
  650.6 19.4 %collective-permute-start.194 = (bf16[8,6144]{1,0:T(8,128)(2,1)S(1)}, bf16[8,6144]{1,0:T(8,128)(2,1)S(1)}, u32[]{:S(2)}, u32[]{:S(2)}) collective-permute-start(bf16[8,6144]{1,0:T(8,128)(2,1)S(1)} %get-tuple-element.721), channel_id=1, source_target_pairs={{0,16},{8,24},{16,0},{24,8},{1,17},{9,25},{17,1},{25,9},{2,18},{10... | collective-permute-start | bytes 294920 | tf_op jit(solution)/shard_map/ppermute | solution.py:32
  670.3 15.8 %collective-permute-start.200 = (bf16[24,6144]{1,0:T(8,128)(2,1)S(1)}, bf16[24,6144]{1,0:T(8,128)(2,1)S(1)}, u32[]{:S(2)}, u32[]{:S(2)}) collective-permute-start(bf16[24,6144]{1,0:T(8,128)(2,1)S(1)} %get-tuple-element.731.refs_0_), channel_id=1, source_target_pairs={{0,2},{2,4},{4,6},{6,0},{1,3},{3,5},{5,7},{7,1},{8,10},{10,12},{12... | collective-permute-start | bytes 884744 | tf_op jit(solution)/shard_map/ppermute | solution.py:32
  670.4 15.7 %collective-permute-start.201 = (bf16[24,6144]{1,0:T(8,128)(2,1)S(1)}, bf16[24,6144]{1,0:T(8,128)(2,1)S(1)}, u32[]{:S(2)}, u32[]{:S(2)}) collective-permute-start(bf16[24,6144]{1,0:T(8,128)(2,1)S(1)} %get-tuple-element.731.refs_0_), channel_id=1, source_target_pairs={{0,4},{2,6},{4,0},{6,2},{1,5},{3,7},{5,1},{7,3},{8,12},{10,14},{12... | collective-permute-start | bytes 884744 | tf_op jit(solution)/shard_map/ppermute | solution.py:32
  690.2 16.6 %collective-permute-start.199 = (bf16[24,6144]{1,0:T(8,128)(2,1)S(1)}, bf16[24,6144]{1,0:T(8,128)(2,1)S(1)}, u32[]{:S(2)}, u32[]{:S(2)}) collective-permute-start(bf16[24,6144]{1,0:T(8,128)(2,1)S(1)} %get-tuple-element.730), channel_id=1, source_target_pairs={{0,2},{2,4},{4,6},{6,0},{1,3},{3,5},{5,7},{7,1},{8,10},{10,12},{12... | collective-permute-start | bytes 884744 | tf_op jit(solution)/shard_map/ppermute | solution.py:32
  712.2 15.6 %collective-permute-start.210 = (bf16[24,6144]{1,0:T(8,128)(2,1)S(1)}, bf16[24,6144]{1,0:T(8,128)(2,1)S(1)}, u32[]{:S(2)}, u32[]{:S(2)}) collective-permute-start(bf16[24,6144]{1,0:T(8,128)(2,1)S(1)} %get-tuple-element.751), channel_id=1, source_target_pairs={{0,2},{2,4},{4,6},{6,0},{1,3},{3,5},{5,7},{7,1},{8,10},{10,12},{12... | collective-permute-start | bytes 884744 | tf_op jit(solution)/shard_map/ppermute | solution.py:32
  (220 other events, 2160.4 us)
